TPU v7x, 512 devices: a whole 4x4x16 slice. The times are simulated.
512 devices in a mesh: group: 16 (over z), ctx: 32 (over x, y, core).
Axes of the slice: x: 4, y: 4, z: 16, core: 2. Of those that a mesh axis runs over, the one named last changes fastest.
Arguments:
- query: bfloat16 [16384, 8192], P('ctx', 'group'), may hold values from -80 to 80
- grad_out: bfloat16 [16384, 8192], P('ctx', 'group'), may hold values from -6 to 6
- key_raw: bfloat16 [1024, 16384], P('group', 'ctx'), may hold values from -4.1 to 4.1
- value_raw: bfloat16 [1024, 16384], P('group', 'ctx'), may hold values from -6 to 6
- beacon_key: bfloat16 [1024, 1024], P('group', 'ctx'), may hold values from -6 to 6
- beacon_value: bfloat16 [1024, 1024], P('group', 'ctx'), may hold values from -6 to 6
- chat_of_span: int32 [32], replicated, may hold values from 0 to 7, never falling along the last dimension, each value on 1 to 17 neighbouring positions
- turn_begin: int32 [16384], P('ctx'), may hold values from 0 to 511, as said below
Outputs:
- grad_query: bfloat16 [16384, 8192], P('ctx', 'group')
- grad_key_raw: float32 [1024, 16384], P('group', 'ctx')
- grad_value_raw: float32 [1024, 16384], P('group', 'ctx')
- grad_beacon_key: float32 [1024, 1024], P('group', 'ctx')
- grad_beacon_value: float32 [1024, 1024], P('group', 'ctx')
Inputs may be any that keep to these rules, and one draw needn't show every extreme that they name: `turn_begin`: 0 at a span's first token, never above the token's own position within its span, never falling within a span; a turn begins at the last token of every span.
All inputs are finite; a program needn't handle non-finite values.
Results may differ from a plain program's by a relative error of at most 0.017.
Values may be sent and summed in bfloat16 or wider, within the bound.
A program may use at most 192 MiB of HBM per device.

v0:
```python
import jax
import jax.numpy as jnp
from jax import lax
from jax.sharding import PartitionSpec as P


def from_partner(block, axis, bit):
    count = lax.axis_size(axis)
    route = []
    for low in range(count):
        high = low | 1 << bit
        if high != low and high < count:
            route += [(low, high), (high, low)]
    return lax.ppermute(block, axis, route)


def take_half(values_in, dim_index, half_index, half_width):
    return lax.dynamic_slice_in_dim(values_in, half_index * half_width, half_width, dim_index)


def reduce_beacons(stacked):
    return lax.psum_scatter(
        stacked.astype(jnp.bfloat16), "ctx", scatter_dimension=2, tiled=True
    ).astype(jnp.float32)


def on_device(
    query, grad_out, key_raw, value_raw, beacon_key, beacon_value, chat_of_span, turn_begin
):
    half_width = key_raw.shape[0]
    head_size = 2 * half_width
    span_len = key_raw.shape[1]
    per_block = beacon_key.shape[1]
    position = lax.axis_index("ctx")
    parity = lax.axis_index("group") % 2
    partner_bit = 1 - parity
    score_scale = head_size ** (-0.5)
    partner = from_partner((key_raw, value_raw, beacon_key, beacon_value), "group", 0)

    def rejoin(mine, theirs):
        lower = jnp.where(parity == 0, mine, theirs)
        upper = jnp.where(parity == 0, theirs, mine)
        return jnp.concatenate([lower, upper], 0)

    keys_local = rejoin(key_raw, partner[0])
    values_local = rejoin(value_raw, partner[1])
    beacon_keys = rejoin(beacon_key, partner[2])
    beacon_values = rejoin(beacon_value, partner[3])
    local_pos = jnp.arange(span_len, dtype=jnp.int32)
    raw_seen = (local_pos[None, :] <= local_pos[:, None]) & (
        local_pos[None, :] >= turn_begin[:, None]
    )
    all_bkeys, all_bvalues = (
        lax.all_gather(beacon_keys, "ctx", axis=1, tiled=True),
        lax.all_gather(beacon_values, "ctx", axis=1, tiled=True),
    )
    beacon_total = all_bkeys.shape[1]
    span_count = beacon_total // per_block
    span_ids = jnp.arange(span_count, dtype=jnp.int32)
    own_chat = jnp.sum(jnp.where(span_ids == position, chat_of_span, 0))
    span_seen = (span_ids < position) & (chat_of_span == own_chat)
    beacon_seen = jnp.repeat(span_seen, per_block)
    visible = jnp.concatenate(
        [jnp.broadcast_to(beacon_seen[None, :], (span_len, beacon_total)), raw_seen], 1
    )
    keys_all = jnp.concatenate([all_bkeys, keys_local], 1)
    values_all = jnp.concatenate([all_bvalues, values_local], 1)
    heads = query.shape[1] // head_size
    grad_keys = jnp.zeros((head_size, beacon_total + span_len), jnp.float32)
    grad_values = jnp.zeros((head_size, beacon_total + span_len), jnp.float32)
    pieces = []
    for head_index in range(heads):
        q_head = query[:, head_index * head_size : (head_index + 1) * head_size]
        d_head = grad_out[:, head_index * head_size : (head_index + 1) * head_size]
        scores = jnp.dot(q_head, keys_all, preferred_element_type=jnp.float32) * score_scale
        scores = jnp.where(visible, scores, -jnp.inf)
        maxima = jnp.max(scores, axis=1, keepdims=True)
        weights = jnp.exp(scores - maxima)
        probs = weights / jnp.sum(weights, axis=1, keepdims=True)
        probs_low = probs.astype(jnp.bfloat16)
        output = lax.dot_general(
            probs_low, values_all, (((1,), (1,)), ((), ())), preferred_element_type=jnp.float32
        )
        grad_p = jnp.dot(d_head, values_all, preferred_element_type=jnp.float32)
        row_delta = jnp.sum(d_head.astype(jnp.float32) * output, axis=1, keepdims=True)
        grad_s = (probs * (grad_p - row_delta)).astype(jnp.bfloat16)
        grad_q = lax.dot_general(
            grad_s, keys_all, (((1,), (1,)), ((), ())), preferred_element_type=jnp.float32
        )
        pieces.append((grad_q * score_scale).astype(jnp.bfloat16))
        grad_keys = (
            grad_keys
            + lax.dot_general(
                q_head, grad_s, (((0,), (0,)), ((), ())), preferred_element_type=jnp.float32
            )
            * score_scale
        )
        grad_values = grad_values + lax.dot_general(
            d_head, probs_low, (((0,), (0,)), ((), ())), preferred_element_type=jnp.float32
        )
    grad_query = jnp.concatenate(pieces, 1)
    raw_keys = grad_keys[:, beacon_total:]
    raw_values = grad_values[:, beacon_total:]
    beacon_grads = jnp.stack([grad_keys[:, :beacon_total], grad_values[:, :beacon_total]])
    received = (
        from_partner(
            take_half(raw_keys, 0, partner_bit, half_width).astype(jnp.bfloat16), "group", 0
        ).astype(jnp.float32),
        from_partner(
            take_half(raw_values, 0, partner_bit, half_width).astype(jnp.bfloat16), "group", 0
        ).astype(jnp.float32),
        from_partner(
            take_half(beacon_grads, 1, partner_bit, half_width).astype(jnp.bfloat16), "group", 0
        ).astype(jnp.float32),
    )
    beacon_half = reduce_beacons(take_half(beacon_grads, 1, parity, half_width) + received[2])
    grad_key_raw = take_half(raw_keys, 0, parity, half_width) + received[0]
    grad_value_raw = take_half(raw_values, 0, parity, half_width) + received[1]
    return (grad_query, grad_key_raw, grad_value_raw, beacon_half[0], beacon_half[1])


def solution(mesh):
    in_specs = (
        P("ctx", "group"),
        P("ctx", "group"),
        P("group", "ctx"),
        P("group", "ctx"),
        P("group", "ctx"),
        P("group", "ctx"),
        P(),
        P("ctx"),
    )
    out_specs = (
        P("ctx", "group"),
        P("group", "ctx"),
        P("group", "ctx"),
        P("group", "ctx"),
        P("group", "ctx"),
    )
    return jax.shard_map(
        on_device, mesh=mesh, in_specs=in_specs, out_specs=out_specs, check_vma=False
    )
```

profile of v0, /device:TPU:1, one launch (start us, length us, event | category | flops | bytes accessed | tf_op | source)
XLA Modules:
  0.0 257.9 jit_solution(11825450051431591757)
XLA Ops:
  7.2 1.0 copy.30
  8.2 4.4 %collective-permute-start.3 = (bf16[64,512]{0,1:T(8,128)(2,1)S(1)}, bf16[64,512]{0,1:T(8,128)(2,1)S(1)}, u32[]{:S(2)}, u32[]{:S(2)}) collective-permute-start(bf16[64,512]{0,1:T(8,128)(2,1)S(1)} %copy.30), channel_id=1, source_target_pairs={{0,32},{32,0},{64,96},{96,64},{128,160},{160,128},{192,224},{224,1... | collective-permute-start | bytes 196616 | tf_op jit(solution)/shard_map/ppermute | solution.py:14
  12.6 1.9 collective-permute-start.2
  14.5 3.4 %collective-permute-start = (bf16[64,32]{0,1:T(8,128)(2,1)}, bf16[64,32]{0,1:T(8,128)(2,1)S(1)}, u32[]{:S(2)}, u32[]{:S(2)}) collective-permute-start(bf16[64,32]{0,1:T(8,128)(2,1)} %param.12), channel_id=1, source_target_pairs={{0,32},{32,0},{64,96},{96,64},{128,160},{160,128},{192,224},{224,1... | collective-permute-start | bytes 12296 | tf_op jit(solution)/shard_map/ppermute | solution.py:14
  17.9 1.0 copy.27
  18.9 1.9 collective-permute-start.1
  20.8 0.8 fusion.39
  21.6 1.1 fusion.68
  22.8 1.3 fusion.58
  24.1 1.3 compare_and_fusion
  26.1 1.3 dynamic-slice
  28.9 28.6 %all_gather.7 = bf16[128,1024]{0,1:T(8,128)(2,1)S(1)} all-gather(bf16[128,32]{0,1:T(8,128)(2,1)S(1)} %pad_maximum_fusion.2), channel_id=1, replica_groups=mesh['group'=16,'ctx'=32] {'ctx'}, dimensions={1}, use_global_device_ids=true | all-gather | bytes 270336 | tf_op jit(solution)/shard_map/all_gather | solution.py:55
  57.5 25.0 %all_gather.6 = bf16[128,1024]{0,1:T(8,128)(2,1)S(1)} all-gather(bf16[128,32]{0,1:T(8,128)(2,1)S(1)} %pad_maximum_fusion.1), channel_id=1, replica_groups=mesh['group'=16,'ctx'=32] {'ctx'}, dimensions={1}, use_global_device_ids=true | all-gather | bytes 270336 | tf_op jit(solution)/shard_map/all_gather | solution.py:54
  86.9 0.8 fusion.19
  91.0 0.8 fusion.16
  93.7 0.8 fusion.17
  96.6 0.8 fusion.18
  101.9 1.9 collective-permute-start.4
  103.9 3.4 %collective-permute-start.6 = (bf16[2,64,1024]{2,1,0:T(8,128)(2,1)S(1)}, bf16[2,64,1024]{2,1,0:T(8,128)(2,1)S(1)}, u32[]{:S(2)}, u32[]{:S(2)}) collective-permute-start(bf16[2,64,1024]{2,1,0:T(8,128)(2,1)S(1)} %fusion.45), channel_id=1, source_target_pairs={{0,32},{32,0},{64,96},{96,64},{128,160},{160,128},{192,224},{224,1... | collective-permute-start | bytes 786440 | tf_op jit(solution)/shard_map/ppermute | solution.py:14
  107.4 1.0 copy.37
  108.4 1.9 collective-permute-start.5
  111.0 2.6 %collective-permute-done.6 = bf16[2,64,1024]{2,1,0:T(8,128)(2,1)S(1)} collective-permute-done((bf16[2,64,1024]{2,1,0:T(8,128)(2,1)S(1)}, bf16[2,64,1024]{2,1,0:T(8,128)(2,1)S(1)}, u32[]{:S(2)}, u32[]{:S(2)}) %collective-permute-start.6) | collective-permute-done | bytes 262176 | tf_op jit(solution)/shard_map/ppermute | solution.py:14
  113.6 1.1 copy.36
  115.6 134.0 %all-reduce.3.cloned.1.call-done = bf16[2,64,1024]{1,0,2:T(2,128)(2,1)} async-done(((bf16[2,64,1024]{1,0,2:T(2,128)(2,1)}), bf16[2,64,1024]{1,0,2:T(2,128)(2,1)}) %all-reduce.3.cloned.1.call-update) | async-done | bytes 262160
  (67 shorter events, 20.6 us)
Async XLA Ops:
  7.2 75.5 %copy-start.1 = (bf16[512,512]{1,0:T(8,128)(2,1)S(1)}, bf16[512,512]{1,0:T(8,128)(2,1)}, u32[]{:S(2)}) copy-start(bf16[512,512]{1,0:T(8,128)(2,1)} %param.8) | copy-start | bytes 1572868
  7.2 242.5 %all-reduce.3.cloned.1.call-start = ((), (), s32[]{:S(2)}) async-start(), calls=%async_computation | async-start | bytes 1048576
  8.2 78.1 %collective-permute-start.3 = (bf16[64,512]{0,1:T(8,128)(2,1)S(1)}, bf16[64,512]{0,1:T(8,128)(2,1)S(1)}, u32[]{:S(2)}, u32[]{:S(2)}) collective-permute-start(bf16[64,512]{0,1:T(8,128)(2,1)S(1)} %copy.30), channel_id=1, source_target_pairs={{0,32},{32,0},{64,96},{96,64},{128,160},{160,128},{192,224},{224,1... | collective-permute-start | bytes 196616 | tf_op jit(solution)/shard_map/ppermute | solution.py:14
  12.6 15.4 %collective-permute-start.2 = (bf16[64,32]{0,1:T(8,128)(2,1)}, bf16[64,32]{0,1:T(8,128)(2,1)S(1)}, u32[]{:S(2)}, u32[]{:S(2)}) collective-permute-start(bf16[64,32]{0,1:T(8,128)(2,1)} %param.13), channel_id=1, source_target_pairs={{0,32},{32,0},{64,96},{96,64},{128,160},{160,128},{192,224},{224,1... | collective-permute-start | bytes 12296 | tf_op jit(solution)/shard_map/ppermute | solution.py:14
  14.5 13.5 %collective-permute-start = (bf16[64,32]{0,1:T(8,128)(2,1)}, bf16[64,32]{0,1:T(8,128)(2,1)S(1)}, u32[]{:S(2)}, u32[]{:S(2)}) collective-permute-start(bf16[64,32]{0,1:T(8,128)(2,1)} %param.12), channel_id=1, source_target_pairs={{0,32},{32,0},{64,96},{96,64},{128,160},{160,128},{192,224},{224,1... | collective-permute-start | bytes 12296 | tf_op jit(solution)/shard_map/ppermute | solution.py:14
  18.9 63.7 %collective-permute-start.1 = (bf16[64,512]{0,1:T(8,128)(2,1)S(1)}, bf16[64,512]{0,1:T(8,128)(2,1)S(1)}, u32[]{:S(2)}, u32[]{:S(2)}) collective-permute-start(bf16[64,512]{0,1:T(8,128)(2,1)S(1)} %copy.27), channel_id=1, source_target_pairs={{0,32},{32,0},{64,96},{96,64},{128,160},{160,128},{192,224},{224,1... | collective-permute-start | bytes 196616 | tf_op jit(solution)/shard_map/ppermute | solution.py:14
  85.7 1.3 copy-start
  101.9 8.3 %collective-permute-start.4 = (bf16[64,512]{1,0:T(8,128)(2,1)S(1)}, bf16[64,512]{1,0:T(8,128)(2,1)S(1)}, u32[]{:S(2)}, u32[]{:S(2)}) collective-permute-start(bf16[64,512]{1,0:T(8,128)(2,1)S(1)} %dynamic-slice_convert_fusion.1), channel_id=1, source_target_pairs={{0,32},{32,0},{64,96},{96,64},{128,160},{160,128},{192,224},{224,1... | collective-permute-start | bytes 196616 | tf_op jit(solution)/shard_map/ppermute | solution.py:14
  103.9 9.6 %collective-permute-start.6 = (bf16[2,64,1024]{2,1,0:T(8,128)(2,1)S(1)}, bf16[2,64,1024]{2,1,0:T(8,128)(2,1)S(1)}, u32[]{:S(2)}, u32[]{:S(2)}) collective-permute-start(bf16[2,64,1024]{2,1,0:T(8,128)(2,1)S(1)} %fusion.45), channel_id=1, source_target_pairs={{0,32},{32,0},{64,96},{96,64},{128,160},{160,128},{192,224},{224,1... | collective-permute-start | bytes 786440 | tf_op jit(solution)/shard_map/ppermute | solution.py:14
  108.4 6.6 %collective-permute-start.5 = (bf16[64,512]{1,0:T(8,128)(2,1)S(1)}, bf16[64,512]{1,0:T(8,128)(2,1)S(1)}, u32[]{:S(2)}, u32[]{:S(2)}) collective-permute-start(bf16[64,512]{1,0:T(8,128)(2,1)S(1)} %dynamic-slice_convert_fusion), channel_id=1, source_target_pairs={{0,32},{32,0},{64,96},{96,64},{128,160},{160,128},{192,224},{224,1... | collective-permute-start | bytes 196616 | tf_op jit(solution)/shard_map/ppermute | solution.py:14
Sparse Core Ops, SparseCore 0:
  114.9 134.7 all-reduce.2
where the time goes:
time: 259 us; the launch traced here: 258 us
  waiting for transfers between devices  137 us (53%)
  blocking collectives  53.6 us (21%)
  starting transfers between devices  18.8 us (7%)
  between operations  15.1 us (6%)
  matrix products  14.7 us (6%)
  other arithmetic  10.8 us (4%)
  local copies, waits for them, and re-layouts  7.91 us (3%)
    unnamed x2, waiting for transfers between devices  134 us
    all_gather x1, blocking collectives, on_device(): lax.all_gather(beacon_values, 'ctx', axis=1, tiled=True)  28.6 us
    all_gather x1, blocking collectives, on_device(): lax.all_gather(beacon_keys, 'ctx', axis=1, tiled=True)  25 us
    ppermute x7, starting transfers between devices, from_partner(): return lax.ppermute(block, axis, route)  18.8 us
    unnamed x13, local copies, waits for them, and re-layouts  5.85 us
  transfers between devices with their start and end apart: 8, of which 3 were waited for; matrix products, arithmetic and copies ran while one was open for 6% of the time, Pallas kernels for 0%

commit v1 on v0

v1 whole, which is shorter than its diff:
```python
import functools
import math

import jax
import jax.numpy as jnp
from jax import lax
from jax.experimental import pallas as pl
from jax.experimental.pallas import tpu as pltpu
from jax.sharding import PartitionSpec as P

MESH = pl.DeviceIdType.MESH
F32 = jnp.float32
BF16 = jnp.bfloat16
HIDDEN = -1e30
BLOCK = 128


def dot(a, b):
    return lax.dot_general(a, b, (((1,), (0,)), ((), ())), preferred_element_type=F32)


def kernel(
    n_ctx,
    window,
    chat_ref,
    q_hbm,
    do_hbm,
    k_hbm,
    v_hbm,
    bk_hbm,
    bv_hbm,
    turn_hbm,
    gq_ref,
    gk_ref,
    gv_ref,
    gbk_ref,
    gbv_ref,
    q,
    do,
    khalf,
    vhalf,
    bkhalf,
    bvhalf,
    turn,
    qt,
    dot_t,
    bias,
    kfull,
    vfull,
    kt,
    vt,
    beacon_out,
    beacon_in,
    mine,
    bkv,
    bkey,
    e_raw,
    e_b,
    dp_raw,
    dp_b,
    p_raw,
    p_b,
    s_raw,
    s_b,
    stats,
    gkt,
    gvt,
    gout,
    gin,
    gb_out,
    gb_in,
    gp_out,
    gp_in,
    load_sem,
    pair_send,
    pair_recv,
    b_send,
    b_recv,
    g_send,
    g_recv,
):
    heads = qt.shape[0]
    span = q.shape[0]
    per = bk_hbm.shape[1]
    half = khalf.shape[0]
    width = 2 * half
    nb = window * per
    blocks = span // BLOCK
    scale = width ** (-0.5)
    factor = scale * math.log2(math.e)

    z = lax.axis_index("group")
    me = lax.axis_index("ctx")
    parity = lax.rem(z, 2)
    partner = z + 1 - 2 * parity

    loads = [
        pltpu.make_async_copy(src, dst, load_sem.at[i])
        for i, (src, dst) in enumerate(
            (
                (bk_hbm, bkhalf),
                (bv_hbm, bvhalf),
                (k_hbm, khalf),
                (v_hbm, vhalf),
                (q_hbm, q),
                (do_hbm, do),
                (turn_hbm, turn),
            )
        )
    ]
    for copy in loads:
        copy.start()

    barrier = pltpu.get_barrier_semaphore()
    pl.semaphore_signal(barrier, inc=1, device_id=(partner, me), device_id_type=MESH)

    def greet(i, carry):
        other = lax.rem(me + i, n_ctx)
        pl.semaphore_signal(barrier, inc=1, device_id=(z, other), device_id_type=MESH)
        return carry

    lax.fori_loop(1, n_ctx, greet, 0)

    loads[0].wait()
    loads[1].wait()
    small = jnp.concatenate(
        [bkhalf[...].astype(F32).T, bvhalf[...].astype(F32).T], axis=1
    )
    beacon_out[...] = small.astype(BF16)
    loads[2].wait()
    loads[3].wait()
    pl.semaphore_wait(barrier, n_ctx)

    def to_partner(i, src, dst):
        return pltpu.make_async_remote_copy(
            src_ref=src,
            dst_ref=dst,
            send_sem=pair_send.at[i],
            recv_sem=pair_recv.at[i],
            device_id=(partner, me),
            device_id_type=MESH,
        )

    pair = [
        to_partner(0, beacon_out, beacon_in),
        to_partner(1, khalf, kfull.at[pl.ds(parity * half, half)]),
        to_partner(2, vhalf, vfull.at[pl.ds(parity * half, half)]),
    ]
    for copy in pair:
        copy.start()

    kfull[pl.ds(parity * half, half), :] = khalf[...]
    vfull[pl.ds(parity * half, half), :] = vhalf[...]

    loads[4].wait()
    loads[5].wait()
    loads[6].wait()
    for h in range(heads):
        qt[h] = q[:, h * width : (h + 1) * width].T
        dot_t[h] = do[:, h * width : (h + 1) * width].T
    begin = turn[...].reshape(1, span)
    rows = lax.broadcasted_iota(jnp.int32, (BLOCK, span), 0)
    cols = lax.broadcasted_iota(jnp.int32, (BLOCK, span), 1)
    for b in range(blocks):
        at = rows + b * BLOCK
        seen = (at <= cols) & (at >= begin)
        bias[b * BLOCK : (b + 1) * BLOCK, :] = jnp.where(seen, 0.0, HIDDEN)

    pair[0].wait_recv()
    own = beacon_out[...]
    other = beacon_in[...]
    low = jnp.where(parity == 0, own, other)
    high = jnp.where(parity == 0, other, own)
    mine[...] = jnp.concatenate(
        [low[:, :half], high[:, :half], low[:, half:], high[:, half:]], axis=1
    )

    def push(i, carry):
        pltpu.make_async_remote_copy(
            src_ref=mine,
            dst_ref=bkv.at[pl.ds(i * per, per)],
            send_sem=b_send,
            recv_sem=b_recv,
            device_id=(z, lax.rem(me + 1 + i, n_ctx)),
            device_id_type=MESH,
        ).start()
        return carry

    lax.fori_loop(0, window, push, 0)

    pair[1].wait_recv()
    kt[...] = kfull[...].T
    pair[2].wait_recv()
    vt[...] = vfull[...].T

    def raw(h, carry):
        top = None
        for b in range(blocks):
            lo, hi = b * BLOCK, (b + 1) * BLOCK
            s = dot(kt[lo:hi, :], qt[h, :, lo:]) * factor + bias[lo:hi, lo:]
            e_raw[h, lo:hi, lo:] = s
            m = jnp.max(s, axis=0, keepdims=True)
            if lo:
                m = jnp.concatenate([jnp.full((1, lo), HIDDEN, F32), m], axis=1)
            top = m if top is None else jnp.maximum(top, m)
        total = jnp.zeros((1, span), F32)
        delta = jnp.zeros((1, span), F32)
        for b in range(blocks):
            lo, hi = b * BLOCK, (b + 1) * BLOCK
            e = jnp.exp2(e_raw[h, lo:hi, lo:] - top[:, lo:])
            e_raw[h, lo:hi, lo:] = e
            g = dot(vt[lo:hi, :], dot_t[h, :, lo:])
            dp_raw[h, lo:hi, lo:] = g
            t = jnp.sum(e, axis=0, keepdims=True)
            d = jnp.sum(e * g, axis=0, keepdims=True)
            if lo:
                zeros = jnp.zeros((1, lo), F32)
                t = jnp.concatenate([zeros, t], axis=1)
                d = jnp.concatenate([zeros, d], axis=1)
            total = total + t
            delta = delta + d
        stats[h, 0:1, :] = top
        stats[h, 1:2, :] = total
        stats[h, 2:3, :] = delta
        return carry

    lax.fori_loop(0, heads, raw, 0)

    pltpu.make_async_copy(bkv, bkv, b_recv).wait()
    bkey[...] = bkv[:, :width].T

    chat = chat_ref[me]

    def beacons(h, carry):
        top_raw = stats[h, 0:1, :]
        top = top_raw
        for i in range(window):
            lo, hi = i * per, (i + 1) * per
            span_id = me - 1 - i
            shown = (span_id >= 0) & (chat_ref[jnp.maximum(span_id, 0)] == chat)
            shift = jnp.where(shown, 0.0, HIDDEN).astype(F32)
            s = dot(bkv[lo:hi, :width], qt[h]) * factor + shift
            e_b[h, lo:hi, :] = s
            top = jnp.maximum(top, jnp.max(s, axis=0, keepdims=True))
        total = jnp.zeros((1, span), F32)
        delta = jnp.zeros((1, span), F32)
        for lo in range(0, nb, 64):
            hi = min(lo + 64, nb)
            e = jnp.exp2(e_b[h, lo:hi, :] - top)
            e_b[h, lo:hi, :] = e
            g = dot(bkv[lo:hi, width:], dot_t[h])
            dp_b[h, lo:hi, :] = g
            total = total + jnp.sum(e, axis=0, keepdims=True)
            delta = delta + jnp.sum(e * g, axis=0, keepdims=True)
        alpha = jnp.exp2(top_raw - top)
        inv = 1.0 / (total + alpha * stats[h, 1:2, :])
        f_raw = alpha * inv
        delta = delta * inv + f_raw * stats[h, 2:3, :]
        for lo in range(0, nb, 64):
            hi = min(lo + 64, nb)
            p = e_b[h, lo:hi, :] * inv
            p_b[h, lo:hi, :] = p.astype(BF16)
            s_b[h, lo:hi, :] = (p * (dp_b[h, lo:hi, :] - delta)).astype(BF16)
        for b in range(blocks):
            lo, hi = b * BLOCK, (b + 1) * BLOCK
            p = e_raw[h, lo:hi, lo:] * f_raw[:, lo:]
            p_raw[h, lo:hi, lo:] = p.astype(BF16)
            s_raw[h, lo:hi, lo:] = (p * (dp_raw[h, lo:hi, lo:] - delta[:, lo:])).astype(BF16)
            if b % 2:
                s_raw[h, lo:hi, lo - BLOCK : lo] = jnp.zeros((BLOCK, BLOCK), BF16)
        return carry

    lax.fori_loop(0, heads, beacons, 0)

    gk_b = jnp.zeros((nb, width), F32)
    gv_b = jnp.zeros((nb, width), F32)
    for h in range(heads):
        gk_b = gk_b + dot(s_b[h], q[:, h * width : (h + 1) * width])
        gv_b = gv_b + dot(p_b[h], do[:, h * width : (h + 1) * width])
    gb_out[:, :width] = (gk_b * scale).astype(BF16)
    gb_out[:, width:] = gv_b.astype(BF16)

    def push_back(i, carry):
        pltpu.make_async_remote_copy(
            src_ref=gb_out.at[pl.ds(i * per, per)],
            dst_ref=gb_in.at[pl.ds(i * per, per)],
            send_sem=g_send,
            recv_sem=g_recv,
            device_id=(z, lax.rem(me + n_ctx - 1 - i, n_ctx)),
            device_id_type=MESH,
        ).start()
        return carry

    lax.fori_loop(0, window, push_back, 0)

    for b in range(blocks):
        lo, hi = b * BLOCK, (b + 1) * BLOCK
        gk = jnp.zeros((BLOCK, width), F32)
        gv = jnp.zeros((BLOCK, width), F32)
        for h in range(heads):
            gk = gk + dot(s_raw[h, lo:hi, lo:], q[lo:, h * width : (h + 1) * width])
            gv = gv + dot(p_raw[h, lo:hi, lo:], do[lo:, h * width : (h + 1) * width])
        gkt[:, lo:hi] = (gk * scale).T
        gvt[:, lo:hi] = gv.T

    mine_at = pl.ds(parity * half, half)
    theirs_at = pl.ds((1 - parity) * half, half)
    gout[0] = gkt[theirs_at, :].astype(BF16)
    gout[1] = gvt[theirs_at, :].astype(BF16)
    pair_g = to_partner(3, gout, gin)
    pair_g.start()

    step = 2 * BLOCK

    def queries(h, carry):
        for lo in range(0, span, step):
            hi = lo + step
            g = dot(kfull[:, :hi], s_raw[h, :hi, lo:hi]) + dot(bkey[...], s_b[h, :, lo:hi])
            gq_ref[lo:hi, pl.ds(h * width, width)] = (g * scale).T.astype(BF16)
        return carry

    for h in range(heads):
        queries(h, 0)

    pltpu.make_async_copy(gb_in, gb_in, g_recv).wait()
    gsum = jnp.zeros((per, 2 * width), F32)
    for i in range(window):
        gsum = gsum + gb_in[i * per : (i + 1) * per, :].astype(F32)
    low = jnp.concatenate([gsum[:, :half], gsum[:, width : width + half]], axis=1)
    high = jnp.concatenate([gsum[:, half:width], gsum[:, width + half :]], axis=1)
    gp_out[...] = jnp.where(parity == 0, high, low).astype(BF16)
    pair_b = to_partner(4, gp_out, gp_in)
    pair_b.start()
    kept = jnp.where(parity == 0, low, high)

    pair_g.wait_recv()
    gk_ref[...] = gkt[mine_at, :] + gin[0].astype(F32)
    gv_ref[...] = gvt[mine_at, :] + gin[1].astype(F32)

    pair_b.wait_recv()
    final = kept + gp_in[...].astype(F32)
    gbk_ref[...] = final[:, :half].T
    gbv_ref[...] = final[:, half:].T

    for copy in pair:
        copy.wait_send()
    pair_g.wait_send()
    pair_b.wait_send()
    pltpu.make_async_copy(bkv, bkv, b_send).wait()
    pltpu.make_async_copy(gb_out, gb_out, g_send).wait()


def on_device(
    n_ctx, query, grad_out, key_raw, value_raw, beacon_key, beacon_value, chat_of_span, turn_begin
):
    span, lanes = query.shape
    half, per = beacon_key.shape
    width = 2 * half
    heads = lanes // width
    window = min(16, n_ctx - 1)
    nb = window * per
    vmem = pltpu.VMEM
    anywhere = pl.BlockSpec(memory_space=pl.ANY)
    dma = pltpu.SemaphoreType.DMA
    return pl.pallas_call(
        functools.partial(kernel, n_ctx, window),
        out_shape=(
            jax.ShapeDtypeStruct((span, lanes), BF16),
            jax.ShapeDtypeStruct((half, span), F32),
            jax.ShapeDtypeStruct((half, span), F32),
            jax.ShapeDtypeStruct((half, per), F32),
            jax.ShapeDtypeStruct((half, per), F32),
        ),
        in_specs=[pl.BlockSpec(memory_space=pltpu.SMEM)] + [anywhere] * 7,
        out_specs=[pl.BlockSpec(memory_space=pltpu.VMEM)] * 5,
        scratch_shapes=[
            vmem((span, lanes), BF16),
            vmem((span, lanes), BF16),
            vmem((half, span), BF16),
            vmem((half, span), BF16),
            vmem((half, per), BF16),
            vmem((half, per), BF16),
            vmem((span,), jnp.int32),
            vmem((heads, width, span), BF16),
            vmem((heads, width, span), BF16),
            vmem((span, span), F32),
            vmem((width, span), BF16),
            vmem((width, span), BF16),
            vmem((span, width), BF16),
            vmem((span, width), BF16),
            vmem((per, width), BF16),
            vmem((per, width), BF16),
            vmem((per, 2 * width), BF16),
            vmem((nb, 2 * width), BF16),
            vmem((width, nb), BF16),
            vmem((heads, span, span), F32),
            vmem((heads, nb, span), F32),
            vmem((heads, span, span), F32),
            vmem((heads, nb, span), F32),
            vmem((heads, span, span), BF16),
            vmem((heads, nb, span), BF16),
            vmem((heads, span, span), BF16),
            vmem((heads, nb, span), BF16),
            vmem((heads, 8, span), F32),
            vmem((width, span), F32),
            vmem((width, span), F32),
            vmem((2, half, span), BF16),
            vmem((2, half, span), BF16),
            vmem((nb, 2 * width), BF16),
            vmem((nb, 2 * width), BF16),
            vmem((per, width), BF16),
            vmem((per, width), BF16),
            dma((7,)),
            dma((5,)),
            dma((5,)),
            dma,
            dma,
            dma,
            dma,
        ],
        compiler_params=pltpu.CompilerParams(
            collective_id=0, has_side_effects=True, vmem_limit_bytes=48 * 1024 * 1024
        ),
        cost_estimate=pl.CostEstimate(
            flops=10 * heads * span * (span + nb) * width,
            bytes_accessed=6 * span * lanes,
            transcendentals=heads * span * (span + nb),
        ),
        name="beacon_backward",
    )(chat_of_span, query, grad_out, key_raw, value_raw, beacon_key, beacon_value, turn_begin)


def solution(mesh):
    in_specs = (
        P("ctx", "group"),
        P("ctx", "group"),
        P("group", "ctx"),
        P("group", "ctx"),
        P("group", "ctx"),
        P("group", "ctx"),
        P(),
        P("ctx"),
    )
    out_specs = (
        P("ctx", "group"),
        P("group", "ctx"),
        P("group", "ctx"),
        P("group", "ctx"),
        P("group", "ctx"),
    )
    return jax.shard_map(
        functools.partial(on_device, mesh.shape["ctx"]),
        mesh=mesh,
        in_specs=in_specs,
        out_specs=out_specs,
        check_vma=False,
    )
```

time: 259 us -> 45.9 us (0.18)
  the two profiles are of different devices: /device:TPU:1 before, /device:TPU:6 now
where the time goes in v1:
time: 45.9 us; the launch traced here: 45.5 us
  Pallas kernels  36.2 us (79%)
  local copies, waits for them, and re-layouts  8.69 us (19%)
  between operations  0.67 us (1%)
    pallas_call x1, Pallas kernels, on_device(): pl.pallas_call(functools.partial(kernel, n_ctx, window), out_shape=(jax.S...  36.2 us
    unnamed x19, local copies, waits for them, and re-layouts  7.33 us
    pallas_call x2, local copies, waits for them, and re-layouts, on_device(): pl.pallas_call(functools.partial(kernel, n_ctx, window), out_shape=(jax.S...  1.36 us

profile of v1, /device:TPU:6, one launch (start us, length us, event | category | flops | bytes accessed | tf_op | source)
XLA Modules:
  0.0 45.5 jit_solution(15900842333762465407)
XLA Ops:
  0.6 0.0 copy-start.6
  0.6 0.8 %copy.13.bk_hbm = bf16[64,32]{1,0:T(8,128)(2,1)S(1)} copy(bf16[64,32]{0,1:T(8,128)(2,1)} %param.12) | data formatting | bytes 8192 | tf_op args[4]
  1.4 0.0 copy-done.6
  1.4 0.0 copy-start.4
  1.5 0.0 copy-start.5
  1.5 0.1 copy.14.bv_hbm
  1.6 0.6 %copy-done.4 = s32[512]{0:T(512)S(1)} copy-done((s32[512]{0:T(512)S(1)}, s32[512]{0:T(512)}, u32[]{:S(2)}) %copy-start.4) | copy-done | bytes 2072
  2.1 0.0 copy-done.5
  2.1 0.0 copy-start
  2.1 1.0 %copy-done = bf16[512,512]{1,0:T(8,128)(2,1)S(1)} copy-done((bf16[512,512]{1,0:T(8,128)(2,1)S(1)}, bf16[512,512]{1,0:T(8,128)(2,1)}, u32[]{:S(2)}) %copy-start) | copy-done | bytes 524312
  3.2 0.0 copy-start.1
  3.2 1.0 %copy-done.1 = bf16[512,512]{1,0:T(8,128)(2,1)S(1)} copy-done((bf16[512,512]{1,0:T(8,128)(2,1)S(1)}, bf16[512,512]{1,0:T(8,128)(2,1)}, u32[]{:S(2)}) %copy-start.1) | copy-done | bytes 524312
  4.2 0.0 copy-start.2
  4.2 0.8 %copy-done.2 = bf16[64,512]{1,0:T(8,128)(2,1)S(1)} copy-done((bf16[64,512]{1,0:T(8,128)(2,1)S(1)}, bf16[64,512]{1,0:T(8,128)(2,1)}, u32[]{:S(2)}) %copy-start.2) | copy-done | bytes 65560
  5.1 0.0 copy-start.3
  5.1 0.8 %copy-done.3 = bf16[64,512]{1,0:T(8,128)(2,1)S(1)} copy-done((bf16[64,512]{1,0:T(8,128)(2,1)S(1)}, bf16[64,512]{1,0:T(8,128)(2,1)}, u32[]{:S(2)}) %copy-start.3) | copy-done | bytes 65560
  5.9 36.2 %beacon_backward.1 = (bf16[512,512]{1,0:T(8,128)(2,1)S(1)}, f32[64,512]{1,0:T(8,128)S(1)}, f32[64,512]{1,0:T(8,128)S(1)}, f32[64,32]{1,0:T(8,128)S(1)}, f32[64,32]{1,0:T(8,128)S(1)}) custom-call(s32[32]{0:T(128)S(1)} %copy-done.5, bf16[512,512]{1,0:T(8,128)(2,1)S(1)} %copy-done, bf16[512,512]{1,0:T(8,128)(2,1)S(1)} %copy-done.1, ...), custom_call_target="tpu_custom_call" | custom-call | flops 2684354560 | bytes 1572864 | tf_op jit(solution)/shard_map/beacon_backward/pallas_call | solution.py:365
  42.1 0.7 %copy.15 = f32[64,32]{0,1:T(8,128)} copy(f32[64,32]{1,0:T(8,128)S(1)} %get-tuple-element.8) | data formatting | bytes 16384 | tf_op jit(solution)/shard_map/beacon_backward/pallas_call | solution.py:365
  42.7 0.7 %copy.16 = f32[64,32]{0,1:T(8,128)} copy(f32[64,32]{1,0:T(8,128)S(1)} %get-tuple-element.9) | data formatting | bytes 16384 | tf_op jit(solution)/shard_map/beacon_backward/pallas_call | solution.py:365
  43.4 0.8 %copy.20 = bf16[512,512]{1,0:T(8,128)(2,1)} copy(bf16[512,512]{1,0:T(8,128)(2,1)S(1)} %get-tuple-element.15) | data formatting | bytes 1048576
  44.2 0.7 %copy.21 = f32[64,512]{1,0:T(8,128)} copy(f32[64,512]{1,0:T(8,128)S(1)} %get-tuple-element.16) | data formatting | bytes 262144
  44.9 0.7 %copy.22 = f32[64,512]{1,0:T(8,128)} copy(f32[64,512]{1,0:T(8,128)S(1)} %get-tuple-element.17) | data formatting | bytes 262144
Async XLA Ops:
  0.6 0.8 %copy-start.6 = (bf16[64,32]{0,1:T(8,128)(2,1)S(1)}, bf16[64,32]{0,1:T(8,128)(2,1)}, u32[]{:S(2)}) copy-start(bf16[64,32]{0,1:T(8,128)(2,1)} %param.13) | copy-start | bytes 12292
  1.4 0.7 %copy-start.4 = (s32[512]{0:T(512)S(1)}, s32[512]{0:T(512)}, u32[]{:S(2)}) copy-start(s32[512]{0:T(512)} %turn_hbm.1) | copy-start | bytes 6148
  1.5 0.7 %copy-start.5 = (s32[32]{0:T(128)S(1)}, s32[32]{0:T(128)}, u32[]{:S(2)}) copy-start(s32[32]{0:T(128)} %chat_ref.1) | copy-start | bytes 388
  2.1 1.0 %copy-start = (bf16[512,512]{1,0:T(8,128)(2,1)S(1)}, bf16[512,512]{1,0:T(8,128)(2,1)}, u32[]{:S(2)}) copy-start(bf16[512,512]{1,0:T(8,128)(2,1)} %q_hbm.1) | copy-start | bytes 1572868
  3.2 1.0 %copy-start.1 = (bf16[512,512]{1,0:T(8,128)(2,1)S(1)}, bf16[512,512]{1,0:T(8,128)(2,1)}, u32[]{:S(2)}) copy-start(bf16[512,512]{1,0:T(8,128)(2,1)} %do_hbm.1) | copy-start | bytes 1572868
  4.2 0.8 %copy-start.2 = (bf16[64,512]{1,0:T(8,128)(2,1)S(1)}, bf16[64,512]{1,0:T(8,128)(2,1)}, u32[]{:S(2)}) copy-start(bf16[64,512]{1,0:T(8,128)(2,1)} %k_hbm.1) | copy-start | bytes 196612
  5.1 0.8 %copy-start.3 = (bf16[64,512]{1,0:T(8,128)(2,1)S(1)}, bf16[64,512]{1,0:T(8,128)(2,1)}, u32[]{:S(2)}) copy-start(bf16[64,512]{1,0:T(8,128)(2,1)} %v_hbm.1) | copy-start | bytes 196612

commit v2 on v0

v2 whole, which is shorter than its diff:
```python
import functools
import math
import types

import jax
import jax.numpy as jnp
from jax import lax
from jax.experimental import pallas as pl
from jax.experimental.pallas import tpu as pltpu
from jax.sharding import PartitionSpec as P

MESH = pl.DeviceIdType.MESH
F32 = jnp.float32
BF16 = jnp.bfloat16
HIDDEN = -1e30
BLOCK = 128
LOG2E = math.log2(math.e)


def dot(a, b):
    return lax.dot_general(a, b, (((1,), (0,)), ((), ())), preferred_element_type=F32)


def head_lanes(h, width):
    return slice(h * width, (h + 1) * width)


def turn_queries(r, d):
    for h in range(d.heads):
        r.qt[h] = r.q[:, head_lanes(h, d.width)].T
        r.dot_t[h] = r.do[:, head_lanes(h, d.width)].T


def hide_tokens(r, d):
    begin = r.turn[...].reshape(1, d.span)
    rows = lax.broadcasted_iota(jnp.int32, (BLOCK, d.span), 0)
    cols = lax.broadcasted_iota(jnp.int32, (BLOCK, d.span), 1)
    for lo in range(0, d.span, BLOCK):
        at = rows + lo
        seen = (at <= cols) & (at >= begin)
        r.bias[lo : lo + BLOCK, :] = jnp.where(seen, 0.0, HIDDEN)


def widen(row, lo, fill):
    if lo == 0:
        return row
    return jnp.concatenate([jnp.full((1, lo), fill, F32), row], axis=1)


def raw_part(r, d, h):
    top = jnp.full((1, d.span), HIDDEN, F32)
    for lo in range(0, d.span, BLOCK):
        hi = lo + BLOCK
        s = dot(r.kt[lo:hi, :], r.qt[h, :, lo:]) * d.factor + r.bias[lo:hi, lo:]
        r.e_raw[h, lo:hi, lo:] = s
        top = jnp.maximum(top, widen(jnp.max(s, axis=0, keepdims=True), lo, HIDDEN))
    total = jnp.zeros((1, d.span), F32)
    delta = jnp.zeros((1, d.span), F32)
    for lo in range(0, d.span, BLOCK):
        hi = lo + BLOCK
        e = jnp.exp2(r.e_raw[h, lo:hi, lo:] - top[:, lo:])
        r.e_raw[h, lo:hi, lo:] = e
        g = dot(r.vt[lo:hi, :], r.dot_t[h, :, lo:])
        r.dp_raw[h, lo:hi, lo:] = g
        total = total + widen(jnp.sum(e, axis=0, keepdims=True), lo, 0.0)
        delta = delta + widen(jnp.sum(e * g, axis=0, keepdims=True), lo, 0.0)
    r.stats[h, 0:1, :] = top
    r.stats[h, 1:2, :] = total
    r.stats[h, 2:3, :] = delta


def blocks_of(d, part):
    base = part * d.nb
    return [(lo, min(lo + BLOCK, base + d.nb)) for lo in range(base, base + d.nb, BLOCK)]


def slot_shifts(r, d, me, part):
    core = lax.rem(me, 2)
    chat = r.chat[me]
    shifts = []
    for k in range(1, d.window + 1):
        if part == 0:
            span_id = me - 2 * k
        elif k < d.window:
            span_id = me + 1 - 2 * core - 2 * k
        else:
            span_id = me - core + (1 - core) * (1 - 2 * k)
        shown = (span_id >= 0) & (r.chat[jnp.maximum(span_id, 0)] == chat)
        shifts.append(jnp.where(shown, 0.0, HIDDEN).astype(F32))
    return shifts


def beacon_part(r, d, h, part, shifts):
    top = jnp.full((1, d.span), HIDDEN, F32)
    for lo, hi in blocks_of(d, part):
        s = dot(r.bkv[lo:hi, : d.width], r.qt[h]) * d.factor
        for at in range(lo, hi, d.per):
            moved = s[at - lo : at - lo + d.per] + shifts[(at - part * d.nb) // d.per]
            r.e_b[h, at : at + d.per, :] = moved
            top = jnp.maximum(top, jnp.max(moved, axis=0, keepdims=True))
    total = jnp.zeros((1, d.span), F32)
    delta = jnp.zeros((1, d.span), F32)
    for lo, hi in blocks_of(d, part):
        e = jnp.exp2(r.e_b[h, lo:hi, :] - top)
        r.e_b[h, lo:hi, :] = e
        g = dot(r.bkv[lo:hi, d.width :], r.dot_t[h])
        r.dp_b[h, lo:hi, :] = g
        total = total + jnp.sum(e, axis=0, keepdims=True)
        delta = delta + jnp.sum(e * g, axis=0, keepdims=True)
    at = 3 * (part + 1)
    r.stats[h, at : at + 1, :] = top
    r.stats[h, at + 1 : at + 2, :] = total
    r.stats[h, at + 2 : at + 3, :] = delta


def combine(r, d, h):
    tops = [r.stats[h, i : i + 1, :] for i in (0, 3, 6)]
    top = jnp.maximum(jnp.maximum(tops[0], tops[1]), tops[2])
    factors = [jnp.exp2(t - top) for t in tops]
    total = jnp.zeros((1, d.span), F32)
    delta = jnp.zeros((1, d.span), F32)
    for i, f in enumerate(factors):
        total = total + f * r.stats[h, 3 * i + 1 : 3 * i + 2, :]
        delta = delta + f * r.stats[h, 3 * i + 2 : 3 * i + 3, :]
    inv = 1.0 / total
    for i, f in enumerate(factors):
        r.stats[h, 9 + i : 10 + i, :] = f * inv
    r.stats[h, 12:13, :] = delta * inv


def beacon_probs(r, d, h, part):
    f = r.stats[h, 10 + part : 11 + part, :]
    delta = r.stats[h, 12:13, :]
    for lo, hi in blocks_of(d, part):
        p = r.e_b[h, lo:hi, :] * f
        r.p_b[h, lo:hi, :] = p.astype(BF16)
        r.s_b[h, lo:hi, :] = (p * (r.dp_b[h, lo:hi, :] - delta)).astype(BF16)


def raw_probs(r, d, h):
    f = r.stats[h, 9:10, :]
    delta = r.stats[h, 12:13, :]
    for lo in range(0, d.span, BLOCK):
        hi = lo + BLOCK
        p = r.e_raw[h, lo:hi, lo:] * f[:, lo:]
        r.p_raw[h, lo:hi, lo:] = p.astype(BF16)
        r.s_raw[h, lo:hi, lo:] = (p * (r.dp_raw[h, lo:hi, lo:] - delta[:, lo:])).astype(BF16)
        if lo % (2 * BLOCK):
            r.s_raw[h, lo:hi, lo - BLOCK : lo] = jnp.zeros((BLOCK, BLOCK), BF16)


def beacon_grads(r, d, part):
    at = slice(part * d.nb, (part + 1) * d.nb)
    gk = jnp.zeros((d.nb, d.width), F32)
    gv = jnp.zeros((d.nb, d.width), F32)
    for h in range(d.heads):
        gk = gk + dot(r.s_b[h, at, :], r.q[:, head_lanes(h, d.width)])
        gv = gv + dot(r.p_b[h, at, :], r.do[:, head_lanes(h, d.width)])
    return gk * d.scale, gv


def grads_to_sibling(r, d):
    gk, gv = beacon_grads(r, d, 1)
    r.x_out[:, : d.width] = gk.astype(BF16)
    r.x_out[:, d.width :] = gv.astype(BF16)


def pack_halves(ref, at, gk, gv, half):
    ref[0, at, :] = jnp.concatenate([gk[:, :half], gv[:, :half]], axis=1).astype(BF16)
    ref[1, at, :] = jnp.concatenate([gk[:, half:], gv[:, half:]], axis=1).astype(BF16)


def raw_key_grads(r, d, lhs, rhs, out, scale):
    for lo in range(0, d.span, BLOCK):
        hi = lo + BLOCK
        g = jnp.zeros((BLOCK, d.width), F32)
        for h in range(d.heads):
            g = g + dot(lhs[h, lo:hi, lo:], rhs[lo:, head_lanes(h, d.width)])
        out[:, lo:hi] = (g * scale).T


def query_grads(r, d, h):
    for lo in range(0, d.span, 2 * BLOCK):
        hi = lo + 2 * BLOCK
        g = dot(r.kfull[:, :hi], r.s_raw[h, :hi, lo:hi]) + dot(r.bkey[...], r.s_b[h, :, lo:hi])
        r.gq[lo:hi, head_lanes(h, d.width)] = (g * d.scale).T.astype(BF16)


def unfold(r, d, part, halves):
    low, high = halves[0], halves[1]
    half = d.half
    r.bkv[part * d.nb : (part + 1) * d.nb, :] = jnp.concatenate(
        [low[:, :half], high[:, :half], low[:, half:], high[:, half:]], axis=1
    )


def each_head(d, step):
    def one(h, carry):
        step(h)
        return carry

    lax.fori_loop(0, d.heads, one, 0)


def wait_for(ref, sem):
    pltpu.make_async_copy(ref, ref, sem).wait()


def kernel(names, d, *refs):
    r = types.SimpleNamespace(**dict(zip(names, refs)))
    per, half, window, n_ctx = d.per, d.half, d.window, d.n_ctx

    z = lax.axis_index("group")
    me = lax.axis_index("ctx")
    parity = lax.rem(z, 2)
    even = z - parity
    partner = z + 1 - 2 * parity
    core = lax.rem(me, 2)
    sibling = me + 1 - 2 * core
    my_rows = pl.ds(parity * half, half)
    their_rows = pl.ds((1 - parity) * half, half)
    shared = pl.ds(0, (window - 1) * per)
    last = pl.ds((window - 1) * per, per)
    beyond = pl.ds(window * per, per)

    loads = [
        pltpu.make_async_copy(src, dst, r.load_sem.at[i])
        for i, (src, dst) in enumerate(
            (
                (r.bk_hbm, r.bkhalf),
                (r.bv_hbm, r.bvhalf),
                (r.k_hbm, r.kfull.at[my_rows]),
                (r.v_hbm, r.vfull.at[my_rows]),
                (r.q_hbm, r.q),
                (r.do_hbm, r.do),
                (r.turn_hbm, r.turn),
                (r.chat_hbm, r.chat),
            )
        )
    ]
    for copy in loads:
        copy.start()

    barrier = pltpu.get_barrier_semaphore()

    def greet(group, ctx):
        pl.semaphore_signal(barrier, inc=1, device_id=(group, ctx), device_id_type=MESH)

    def greet_earlier(i, carry):
        k = window - i // 2
        greet(even + lax.rem(i, 2), lax.rem(me + n_ctx - 2 * k, n_ctx))
        return carry

    lax.fori_loop(0, 2 * window, greet_earlier, 0)
    greet(partner, me)
    greet(z, sibling)
    greet(partner, sibling)

    loads[0].wait()
    loads[1].wait()
    r.beacon_out[...] = jnp.concatenate([r.bkhalf[...], r.bvhalf[...]], axis=1)
    loads[2].wait()
    loads[3].wait()
    pl.semaphore_wait(barrier, 2 * window + 3)

    def remote(src, dst, send, recv, group, ctx):
        return pltpu.make_async_remote_copy(
            src_ref=src,
            dst_ref=dst,
            send_sem=send,
            recv_sem=recv,
            device_id=(group, ctx),
            device_id_type=MESH,
        )

    def to_partner(i, src, dst):
        return remote(src, dst, r.pair_send.at[i], r.pair_recv.at[i], partner, me)

    def to_sibling(i, src, dst):
        return remote(src, dst, r.core_send.at[i], r.core_recv.at[i], z, sibling)

    pair = [
        to_partner(0, r.kfull.at[my_rows], r.kfull.at[my_rows]),
        to_partner(1, r.vfull.at[my_rows], r.vfull.at[my_rows]),
        to_partner(2, r.gout.at[0], r.gin.at[0]),
        to_partner(3, r.gout.at[1], r.gin.at[1]),
    ]
    cores = [
        to_sibling(0, r.b_in.at[:, shared], r.b_sib.at[:, shared]),
        to_sibling(1, r.b_in.at[:, last], r.b_sib.at[:, last]),
        to_sibling(2, r.x_out.at[shared], r.x_in.at[shared]),
        to_sibling(3, r.x_out.at[last], r.x_in.at[last]),
    ]

    pair[0].start()

    def push(i, carry):
        k = window - i // 2
        remote(
            r.beacon_out,
            r.b_in.at[parity, pl.ds((k - 1) * per, per)],
            r.b_send,
            r.b_recv,
            even + lax.rem(i, 2),
            lax.rem(me + 2 * k, n_ctx),
        ).start()
        return carry

    lax.fori_loop(0, 2 * window, push, 0)
    pair[1].start()

    own_chip = [
        remote(
            r.beacon_out,
            r.b_sib.at[parity, last],
            r.own_send.at[i],
            r.own_recv,
            group,
            sibling,
        )
        for i, group in enumerate((z, partner))
    ]

    @pl.when(core == 0)
    def _():
        for copy in own_chip:
            copy.start()

    for i in (4, 5, 6, 7):
        loads[i].wait()
    turn_queries(r, d)
    hide_tokens(r, d)

    @pl.when(core == 0)
    def _():
        r.x_in[last, :] = jnp.zeros((per, 2 * d.width), BF16)

    @pl.when(core == 1)
    def _():
        r.red[:, beyond, :] = jnp.zeros((2, per, d.width), BF16)

    wait_for(r.b_in, r.b_recv)
    cores[0].start()

    @pl.when(core == 1)
    def _():
        cores[1].start()

    pair[0].wait_recv()
    r.kt[...] = r.kfull[...].T
    pair[1].wait_recv()
    r.vt[...] = r.vfull[...].T
    each_head(d, lambda h: raw_part(r, d, h))

    unfold(r, d, 0, r.b_in)
    shifts = slot_shifts(r, d, me, 0)
    each_head(d, lambda h: beacon_part(r, d, h, 0, shifts))

    cores[0].wait_recv()

    @pl.when(core == 0)
    def _():
        cores[1].wait_recv()

    @pl.when(core == 1)
    def _():
        wait_for(r.b_sib.at[:, last], r.own_recv)

    unfold(r, d, 1, r.b_sib)
    shifts_sib = slot_shifts(r, d, me, 1)

    def second(h):
        beacon_part(r, d, h, 1, shifts_sib)
        combine(r, d, h)
        beacon_probs(r, d, h, 1)

    each_head(d, second)
    grads_to_sibling(r, d)
    cores[2].start()

    @pl.when(core == 0)
    def _():
        cores[3].start()

    tail = r.x_out[last, :]
    pack_halves(r.own_out, slice(None), tail[:, : d.width], tail[:, d.width :], half)
    own_back = [
        remote(
            r.own_out.at[p],
            r.red.at[parity, beyond],
            r.back_send.at[p],
            r.back_recv,
            even + p,
            sibling,
        )
        for p in range(2)
    ]

    @pl.when(core == 1)
    def _():
        for copy in own_back:
            copy.start()

    each_head(d, lambda h: beacon_probs(r, d, h, 0))
    gk, gv = beacon_grads(r, d, 0)
    cores[2].wait_recv()

    @pl.when(core == 1)
    def _():
        cores[3].wait_recv()

    gk = gk + r.x_in[:, : d.width].astype(F32)
    gv = gv + r.x_in[:, d.width :].astype(F32)
    pack_halves(r.g_out, slice(None), gk, gv, half)

    def push_back(i, carry):
        k = window - i // 2
        p = lax.rem(i, 2)
        at = pl.ds((k - 1) * per, per)
        remote(
            r.g_out.at[p, at],
            r.red.at[parity, at],
            r.g_send,
            r.g_recv,
            even + p,
            lax.rem(me + n_ctx - 2 * k, n_ctx),
        ).start()
        return carry

    lax.fori_loop(0, 2 * window, push_back, 0)

    each_head(d, lambda h: raw_probs(r, d, h))
    raw_key_grads(r, d, r.p_raw, r.do, r.gvt, 1.0)
    r.gout[1] = r.gvt[their_rows, :].astype(BF16)
    pair[3].start()
    raw_key_grads(r, d, r.s_raw, r.q, r.gkt, d.scale)
    r.gout[0] = r.gkt[their_rows, :].astype(BF16)
    pair[2].start()

    r.bkey[...] = r.bkv[:, : d.width].T
    for h in range(d.heads):
        query_grads(r, d, h)

    whole = pl.ds(0, window * per)
    wait_for(r.red.at[:, whole], r.g_recv)

    @pl.when(core == 0)
    def _():
        wait_for(r.red.at[:, beyond], r.back_recv)

    total = jnp.zeros((per, d.width), F32)
    for p in range(2):
        for k in range(window + 1):
            total = total + r.red[p, k * per : (k + 1) * per, :].astype(F32)
    r.gbk[...] = total[:, :half]
    r.gbv[...] = total[:, half:]

    pair[3].wait_recv()
    r.gv[...] = r.gvt[my_rows, :] + r.gin[1].astype(F32)
    pair[2].wait_recv()
    r.gk[...] = r.gkt[my_rows, :] + r.gin[0].astype(F32)

    for copy in pair:
        copy.wait_send()
    cores[0].wait_send()
    cores[2].wait_send()

    @pl.when(core == 0)
    def _():
        cores[3].wait_send()
        for copy in own_chip:
            copy.wait_send()

    @pl.when(core == 1)
    def _():
        cores[1].wait_send()
        for copy in own_back:
            copy.wait_send()

    wait_for(r.b_in, r.b_send)
    wait_for(r.g_out, r.g_send)


def write_out(*refs):
    sources, results, sems = refs[:5], refs[5:10], refs[10]
    copies = [
        pltpu.make_async_copy(s, o, sems.at[i]) for i, (s, o) in enumerate(zip(sources, results))
    ]
    for copy in copies:
        copy.start()
    for copy in copies:
        copy.wait()


def dims(n_ctx, span, lanes, half, per):
    width = 2 * half
    window = min(8, n_ctx // 2 - 1)
    return types.SimpleNamespace(
        n_ctx=n_ctx,
        span=span,
        lanes=lanes,
        half=half,
        per=per,
        width=width,
        heads=lanes // width,
        window=window,
        nb=window * per,
        scale=width ** (-0.5),
        factor=width ** (-0.5) * LOG2E,
    )


def scratch(d):
    vmem = pltpu.VMEM
    dma = pltpu.SemaphoreType.DMA
    return dict(
        q=vmem((d.span, d.lanes), BF16),
        do=vmem((d.span, d.lanes), BF16),
        bkhalf=vmem((d.per, d.half), BF16),
        bvhalf=vmem((d.per, d.half), BF16),
        turn=vmem((d.span,), jnp.int32),
        chat=pltpu.SMEM((d.n_ctx,), jnp.int32),
        qt=vmem((d.heads, d.width, d.span), BF16),
        dot_t=vmem((d.heads, d.width, d.span), BF16),
        bias=vmem((d.span, d.span), F32),
        kfull=vmem((d.width, d.span), BF16),
        vfull=vmem((d.width, d.span), BF16),
        kt=vmem((d.span, d.width), BF16),
        vt=vmem((d.span, d.width), BF16),
        beacon_out=vmem((d.per, d.width), BF16),
        b_in=vmem((2, d.nb, d.width), BF16),
        b_sib=vmem((2, d.nb, d.width), BF16),
        bkv=vmem((2 * d.nb, 2 * d.width), BF16),
        bkey=vmem((d.width, 2 * d.nb), BF16),
        e_raw=vmem((d.heads, d.span, d.span), F32),
        e_b=vmem((d.heads, 2 * d.nb, d.span), F32),
        dp_raw=vmem((d.heads, d.span, d.span), F32),
        dp_b=vmem((d.heads, 2 * d.nb, d.span), F32),
        p_raw=vmem((d.heads, d.span, d.span), BF16),
        p_b=vmem((d.heads, 2 * d.nb, d.span), BF16),
        s_raw=vmem((d.heads, d.span, d.span), BF16),
        s_b=vmem((d.heads, 2 * d.nb, d.span), BF16),
        stats=vmem((d.heads, 16, d.span), F32),
        gkt=vmem((d.width, d.span), F32),
        gvt=vmem((d.width, d.span), F32),
        gout=vmem((2, d.half, d.span), BF16),
        gin=vmem((2, d.half, d.span), BF16),
        x_out=vmem((d.nb, 2 * d.width), BF16),
        x_in=vmem((d.nb, 2 * d.width), BF16),
        own_out=vmem((2, d.per, d.width), BF16),
        g_out=vmem((2, d.nb, d.width), BF16),
        red=vmem((2, d.nb + d.per, d.width), BF16),
        load_sem=dma((8,)),
        pair_send=dma((4,)),
        pair_recv=dma((4,)),
        core_send=dma((4,)),
        core_recv=dma((4,)),
        own_send=dma((2,)),
        own_recv=dma,
        back_send=dma((2,)),
        back_recv=dma,
        b_send=dma,
        b_recv=dma,
        g_send=dma,
        g_recv=dma,
    )


IN_NAMES = ("chat_hbm", "q_hbm", "do_hbm", "k_hbm", "v_hbm", "bk_hbm", "bv_hbm", "turn_hbm")
OUT_NAMES = ("gq", "gk", "gv", "gbk", "gbv")


def on_device(
    n_ctx, query, grad_out, key_raw, value_raw, beacon_key, beacon_value, chat_of_span, turn_begin
):
    span, lanes = query.shape
    half, per = beacon_key.shape
    d = dims(n_ctx, span, lanes, half, per)
    space = scratch(d)
    hbm = pl.BlockSpec(memory_space=pltpu.HBM)
    vmem = pl.BlockSpec(memory_space=pltpu.VMEM)
    shapes = (
        jax.ShapeDtypeStruct((span, lanes), BF16),
        jax.ShapeDtypeStruct((half, span), F32),
        jax.ShapeDtypeStruct((half, span), F32),
        jax.ShapeDtypeStruct((per, half), F32),
        jax.ShapeDtypeStruct((per, half), F32),
    )
    operands = (
        chat_of_span,
        query,
        grad_out,
        key_raw,
        value_raw,
        beacon_key.T,
        beacon_value.T,
        turn_begin,
    )
    results = pl.pallas_call(
        functools.partial(kernel, IN_NAMES + OUT_NAMES + tuple(space), d),
        out_shape=shapes,
        in_specs=[hbm] * 8,
        out_specs=[vmem] * 5,
        scratch_shapes=list(space.values()),
        compiler_params=pltpu.CompilerParams(
            collective_id=0, has_side_effects=True, vmem_limit_bytes=48 * 1024 * 1024
        ),
        cost_estimate=pl.CostEstimate(
            flops=10 * d.heads * span * (span + 2 * d.nb) * d.width,
            bytes_accessed=6 * span * lanes,
            transcendentals=d.heads * span * (span + 2 * d.nb),
        ),
        name="beacon_backward",
    )(*[pltpu.with_memory_space_constraint(a, pltpu.HBM) for a in operands])
    results = pl.pallas_call(
        write_out,
        out_shape=shapes,
        in_specs=[vmem] * 5,
        out_specs=[hbm] * 5,
        scratch_shapes=[pltpu.SemaphoreType.DMA((5,))],
        name="write_out",
    )(*results)
    return (*results[:3], results[3].T, results[4].T)


def solution(mesh):
    in_specs = (
        P("ctx", "group"),
        P("ctx", "group"),
        P("group", "ctx"),
        P("group", "ctx"),
        P("group", "ctx"),
        P("group", "ctx"),
        P(),
        P("ctx"),
    )
    out_specs = (
        P("ctx", "group"),
        P("group", "ctx"),
        P("group", "ctx"),
        P("group", "ctx"),
        P("group", "ctx"),
    )
    return jax.shard_map(
        functools.partial(on_device, mesh.shape["ctx"]),
        mesh=mesh,
        in_specs=in_specs,
        out_specs=out_specs,
        check_vma=False,
    )
```

time: 259 us -> 36.4 us (0.14)
  waiting for transfers between devices: 137 us -> 0 us
  blocking collectives: 53.6 us -> 0 us
  Pallas kernels: 0 us -> 32.3 us
  starting transfers between devices: 18.8 us -> 0 us
  matrix products: 14.7 us -> 0 us
  between operations: 15.1 us -> 0.65 us
  other arithmetic: 10.8 us -> 0 us
  local copies, waits for them, and re-layouts: 7.91 us -> 3.27 us
    unnamed x2 -> x0, waiting for transfers between devices: 134 us -> none
    all_gather x2 -> x0, blocking collectives: 53.6 us -> none  [the longest x1 28.6 us: on_device(): lax.all_gather(beacon_values, 'ctx', axis=1, tiled=True)]
    pallas_call x0 -> x2, Pallas kernels: none -> 32.3 us  [the longest x1 30.2 us: on_device(): pl.pallas_call(functools.partial(kernel, IN_NAMES + OUT_NAMES + tuple(spa...]
    ppermute x7 -> x0, starting transfers between devices: 18.8 us -> none  [from_partner(): return lax.ppermute(block, axis, route)]
    dot_general x24 -> x0, matrix products: 14.7 us -> none  [the longest x4 3.24 us: on_device(): grad_p = jnp.dot(d_head, values_all, preferred_element_type=jnp.float32)]
    reduce_sum x5 -> x0, other arithmetic: 3.29 us -> none  [the longest x4 1.99 us: on_device(): probs = weights / jnp.sum(weights, axis=1, keepdims=True)]
    convert_element_type x7 -> x0, other arithmetic: 2.87 us -> none  [the longest x4 2.05 us: on_device(): probs_low = probs.astype(jnp.bfloat16)]
    ppermute x7 -> x0, waiting for transfers between devices: 2.82 us -> none  [from_partner(): return lax.ppermute(block, axis, route)]
  transfers between devices with their start and end apart: 8 -> 0, of which waited for: 3 -> 0; matrix products, arithmetic and copies ran while one was open for 6% -> 0% of each run, Pallas kernels for 0% -> 0%
where the time goes in v2:
time: 36.4 us; the launch traced here: 36.2 us
  Pallas kernels  32.3 us (89%)
  local copies, waits for them, and re-layouts  3.27 us (9%)
  between operations  0.65 us (2%)
    pallas_call x1, Pallas kernels, on_device(): pl.pallas_call(functools.partial(kernel, IN_NAMES + OUT_NAMES + tuple(spa...  30.2 us
    unnamed x10, local copies, waits for them, and re-layouts  3.27 us
    pallas_call x1, Pallas kernels, on_device(): pl.pallas_call(write_out, out_shape=shapes, in_specs=[vmem] * 5, out_spec...  2.07 us

profile of v2, /device:TPU:1, one launch (start us, length us, event | category | flops | bytes accessed | tf_op | source)
XLA Modules:
  0.0 36.2 jit_solution(16021594322298815093)
XLA Ops:
  0.6 30.2 %beacon_backward.1 = (bf16[512,512]{1,0:T(8,128)(2,1)S(1)}, f32[64,512]{1,0:T(8,128)S(1)}, f32[64,512]{1,0:T(8,128)S(1)}, f32[32,64]{1,0:T(8,128)S(1)}, f32[32,64]{1,0:T(8,128)S(1)}) custom-call(s32[32]{0:T(128)} %refs_0_.1, bf16[512,512]{1,0:T(8,128)(2,1)} %refs_1_.1, bf16[512,512]{1,0:T(8,128)(2,1)} %refs_2_.1, bf16[64,512]{1,0:T(8,128)(2,1)} %refs_3_.1, ...), custom_call_target="tpu_custom_call" | custom-call | flops 2684354560 | bytes 1572864 | tf_op jit(solution)/shard_map/beacon_backward/pallas_call | solution.py:599
  30.8 0.0 copy-start
  30.8 0.8 %copy-done = bf16[512,512]{1,0:T(8,128)(2,1)} copy-done((bf16[512,512]{1,0:T(8,128)(2,1)}, bf16[512,512]{1,0:T(8,128)(2,1)S(1)}, u32[]{:S(2)}) %copy-start) | copy-done | bytes 524312
  31.6 0.0 copy-start.1
  31.6 0.6 %copy-done.1 = f32[64,512]{1,0:T(8,128)} copy-done((f32[64,512]{1,0:T(8,128)}, f32[64,512]{1,0:T(8,128)S(1)}, u32[]{:S(2)}) %copy-start.1) | copy-done | bytes 131096
  32.3 0.0 copy-start.2
  32.3 0.6 %copy-done.2 = f32[64,512]{1,0:T(8,128)} copy-done((f32[64,512]{1,0:T(8,128)}, f32[64,512]{1,0:T(8,128)S(1)}, u32[]{:S(2)}) %copy-start.2) | copy-done | bytes 131096
  32.9 0.0 copy-start.3
  32.9 0.6 %copy-done.3 = f32[32,64]{1,0:T(8,128)} copy-done((f32[32,64]{1,0:T(8,128)}, f32[32,64]{1,0:T(8,128)S(1)}, u32[]{:S(2)}) %copy-start.3) | copy-done | bytes 8216
  33.5 0.0 copy-start.4
  33.5 0.6 %copy-done.4 = f32[32,64]{1,0:T(8,128)} copy-done((f32[32,64]{1,0:T(8,128)}, f32[32,64]{1,0:T(8,128)S(1)}, u32[]{:S(2)}) %copy-start.4) | copy-done | bytes 8216
  34.1 2.1 %write_out.1 = (bf16[512,512]{1,0:T(8,128)(2,1)}, f32[64,512]{1,0:T(8,128)}, f32[64,512]{1,0:T(8,128)}, f32[32,64]{1,0:T(8,128)}, f32[32,64]{1,0:T(8,128)}) custom-call(bf16[512,512]{1,0:T(8,128)(2,1)} %copy-done, f32[64,512]{1,0:T(8,128)} %copy-done.1, f32[64,512]{1,0:T(8,128)} %copy-done.2, f32[32,64]{1,0:T(8,128)} %copy-done.3, f32[32,64]{1,0:T(8,128)} %copy-done.4), custom_call_target="tpu_custom_call" | custom-call | tf_op jit(solution)/shard_map/write_out/pallas_call | solution.py:615
Async XLA Ops:
  30.8 0.8 %copy-start = (bf16[512,512]{1,0:T(8,128)(2,1)}, bf16[512,512]{1,0:T(8,128)(2,1)S(1)}, u32[]{:S(2)}) copy-start(bf16[512,512]{1,0:T(8,128)(2,1)S(1)} %get-tuple-element.15.refs_0_) | copy-start | bytes 1572868
  31.6 0.6 %copy-start.1 = (f32[64,512]{1,0:T(8,128)}, f32[64,512]{1,0:T(8,128)S(1)}, u32[]{:S(2)}) copy-start(f32[64,512]{1,0:T(8,128)S(1)} %get-tuple-element.16.refs_1_) | copy-start | bytes 393220
  32.3 0.6 %copy-start.2 = (f32[64,512]{1,0:T(8,128)}, f32[64,512]{1,0:T(8,128)S(1)}, u32[]{:S(2)}) copy-start(f32[64,512]{1,0:T(8,128)S(1)} %get-tuple-element.17.refs_2_) | copy-start | bytes 393220
  32.9 0.6 %copy-start.3 = (f32[32,64]{1,0:T(8,128)}, f32[32,64]{1,0:T(8,128)S(1)}, u32[]{:S(2)}) copy-start(f32[32,64]{1,0:T(8,128)S(1)} %get-tuple-element.18.refs_3_) | copy-start | bytes 24580
  33.5 0.6 %copy-start.4 = (f32[32,64]{1,0:T(8,128)}, f32[32,64]{1,0:T(8,128)S(1)}, u32[]{:S(2)}) copy-start(f32[32,64]{1,0:T(8,128)S(1)} %get-tuple-element.19.refs_4_) | copy-start | bytes 24580

commit v3 on v2

--- a/solution.py
+++ b/solution.py
@@ -128,41 +128,17 @@
     r.stats[h, 12:13, :] = delta * inv
 
 
-def beacon_probs(r, d, h, part):
-    f = r.stats[h, 10 + part : 11 + part, :]
-    delta = r.stats[h, 12:13, :]
+def beacon_grads(r, d, part):
     for lo, hi in blocks_of(d, part):
-        p = r.e_b[h, lo:hi, :] * f
-        r.p_b[h, lo:hi, :] = p.astype(BF16)
-        r.s_b[h, lo:hi, :] = (p * (r.dp_b[h, lo:hi, :] - delta)).astype(BF16)
-
-
-def raw_probs(r, d, h):
-    f = r.stats[h, 9:10, :]
-    delta = r.stats[h, 12:13, :]
-    for lo in range(0, d.span, BLOCK):
-        hi = lo + BLOCK
-        p = r.e_raw[h, lo:hi, lo:] * f[:, lo:]
-        r.p_raw[h, lo:hi, lo:] = p.astype(BF16)
-        r.s_raw[h, lo:hi, lo:] = (p * (r.dp_raw[h, lo:hi, lo:] - delta[:, lo:])).astype(BF16)
-        if lo % (2 * BLOCK):
-            r.s_raw[h, lo:hi, lo - BLOCK : lo] = jnp.zeros((BLOCK, BLOCK), BF16)
-
-
-def beacon_grads(r, d, part):
-    at = slice(part * d.nb, (part + 1) * d.nb)
-    gk = jnp.zeros((d.nb, d.width), F32)
-    gv = jnp.zeros((d.nb, d.width), F32)
-    for h in range(d.heads):
-        gk = gk + dot(r.s_b[h, at, :], r.q[:, head_lanes(h, d.width)])
-        gv = gv + dot(r.p_b[h, at, :], r.do[:, head_lanes(h, d.width)])
-    return gk * d.scale, gv
-
-
-def grads_to_sibling(r, d):
-    gk, gv = beacon_grads(r, d, 1)
-    r.x_out[:, : d.width] = gk.astype(BF16)
-    r.x_out[:, d.width :] = gv.astype(BF16)
+        gk = jnp.zeros((hi - lo, d.width), F32)
+        gv = jnp.zeros((hi - lo, d.width), F32)
+        for h in range(d.heads):
+            p = r.e_b[h, lo:hi, :] * r.stats[h, 10 + part : 11 + part, :]
+            s = (p * (r.dp_b[h, lo:hi, :] - r.stats[h, 12:13, :])).astype(BF16)
+            r.s_b[h, lo:hi, :] = s
+            gk = gk + dot(s, r.q[:, head_lanes(h, d.width)])
+            gv = gv + dot(p.astype(BF16), r.do[:, head_lanes(h, d.width)])
+        yield lo - part * d.nb, hi - part * d.nb, gk * d.scale, gv
 
 
 def pack_halves(ref, at, gk, gv, half):
@@ -170,13 +146,20 @@
     ref[1, at, :] = jnp.concatenate([gk[:, half:], gv[:, half:]], axis=1).astype(BF16)
 
 
-def raw_key_grads(r, d, lhs, rhs, out, scale):
-    for lo in range(0, d.span, BLOCK):
-        hi = lo + BLOCK
-        g = jnp.zeros((BLOCK, d.width), F32)
-        for h in range(d.heads):
-            g = g + dot(lhs[h, lo:hi, lo:], rhs[lo:, head_lanes(h, d.width)])
-        out[:, lo:hi] = (g * scale).T
+def raw_grads(r, d, lo):
+    hi = lo + BLOCK
+    gk = jnp.zeros((BLOCK, d.width), F32)
+    gv = jnp.zeros((BLOCK, d.width), F32)
+    for h in range(d.heads):
+        p = r.e_raw[h, lo:hi, lo:] * r.stats[h, 9:10, lo:]
+        s = (p * (r.dp_raw[h, lo:hi, lo:] - r.stats[h, 12:13, lo:])).astype(BF16)
+        r.s_raw[h, lo:hi, lo:] = s
+        if lo % (2 * BLOCK):
+            r.s_raw[h, lo:hi, lo - BLOCK : lo] = jnp.zeros((BLOCK, BLOCK), BF16)
+        gk = gk + dot(s, r.q[lo:, head_lanes(h, d.width)])
+        gv = gv + dot(p.astype(BF16), r.do[lo:, head_lanes(h, d.width)])
+    r.gkt[:, lo:hi] = (gk * d.scale).T
+    r.gvt[:, lo:hi] = gv.T
 
 
 def query_grads(r, d, h):
@@ -192,14 +175,6 @@
     r.bkv[part * d.nb : (part + 1) * d.nb, :] = jnp.concatenate(
         [low[:, :half], high[:, :half], low[:, half:], high[:, half:]], axis=1
     )
-
-
-def each_head(d, step):
-    def one(h, carry):
-        step(h)
-        return carry
-
-    lax.fori_loop(0, d.heads, one, 0)
 
 
 def wait_for(ref, sem):
@@ -222,6 +197,21 @@
     shared = pl.ds(0, (window - 1) * per)
     last = pl.ds((window - 1) * per, per)
     beyond = pl.ds(window * per, per)
+
+    barrier = pltpu.get_barrier_semaphore()
+
+    def greet(group, ctx):
+        pl.semaphore_signal(barrier, inc=1, device_id=(group, ctx), device_id_type=MESH)
+
+    def greet_earlier(i, carry):
+        k = window - i // 2
+        greet(even + lax.rem(i, 2), lax.rem(me + n_ctx - 2 * k, n_ctx))
+        return carry
+
+    lax.fori_loop(0, 2 * window, greet_earlier, 0)
+    greet(partner, me)
+    greet(z, sibling)
+    greet(partner, sibling)
 
     loads = [
         pltpu.make_async_copy(src, dst, r.load_sem.at[i])
@@ -241,21 +231,6 @@
     for copy in loads:
         copy.start()
 
-    barrier = pltpu.get_barrier_semaphore()
-
-    def greet(group, ctx):
-        pl.semaphore_signal(barrier, inc=1, device_id=(group, ctx), device_id_type=MESH)
-
-    def greet_earlier(i, carry):
-        k = window - i // 2
-        greet(even + lax.rem(i, 2), lax.rem(me + n_ctx - 2 * k, n_ctx))
-        return carry
-
-    lax.fori_loop(0, 2 * window, greet_earlier, 0)
-    greet(partner, me)
-    greet(z, sibling)
-    greet(partner, sibling)
-
     loads[0].wait()
     loads[1].wait()
     r.beacon_out[...] = jnp.concatenate([r.bkhalf[...], r.bvhalf[...]], axis=1)
@@ -282,8 +257,13 @@
     pair = [
         to_partner(0, r.kfull.at[my_rows], r.kfull.at[my_rows]),
         to_partner(1, r.vfull.at[my_rows], r.vfull.at[my_rows]),
-        to_partner(2, r.gout.at[0], r.gin.at[0]),
-        to_partner(3, r.gout.at[1], r.gin.at[1]),
+    ]
+    raw_blocks = range(0, d.span, BLOCK)
+    pair_back = [
+        to_partner(
+            2 + i, r.gout.at[:, :, pl.ds(lo, BLOCK)], r.gin.at[:, :, pl.ds(lo, BLOCK)]
+        )
+        for i, lo in enumerate(raw_blocks)
     ]
     cores = [
         to_sibling(0, r.b_in.at[:, shared], r.b_sib.at[:, shared]),
@@ -339,22 +319,24 @@
     def _():
         r.red[:, beyond, :] = jnp.zeros((2, per, d.width), BF16)
 
-    wait_for(r.b_in, r.b_recv)
-    cores[0].start()
-
-    @pl.when(core == 1)
-    def _():
-        cores[1].start()
-
     pair[0].wait_recv()
     r.kt[...] = r.kfull[...].T
     pair[1].wait_recv()
     r.vt[...] = r.vfull[...].T
-    each_head(d, lambda h: raw_part(r, d, h))
+    for h in range(d.heads):
+        raw_part(r, d, h)
+
+    wait_for(r.b_in, r.b_recv)
+    cores[0].start()
+
+    @pl.when(core == 1)
+    def _():
+        cores[1].start()
 
     unfold(r, d, 0, r.b_in)
     shifts = slot_shifts(r, d, me, 0)
-    each_head(d, lambda h: beacon_part(r, d, h, 0, shifts))
+    for h in range(d.heads):
+        beacon_part(r, d, h, 0, shifts)
 
     cores[0].wait_recv()
 
@@ -369,13 +351,13 @@
     unfold(r, d, 1, r.b_sib)
     shifts_sib = slot_shifts(r, d, me, 1)
 
-    def second(h):
+    for h in range(d.heads):
         beacon_part(r, d, h, 1, shifts_sib)
         combine(r, d, h)
-        beacon_probs(r, d, h, 1)
-
-    each_head(d, second)
-    grads_to_sibling(r, d)
+
+    for lo, hi, gk, gv in beacon_grads(r, d, 1):
+        r.x_out[lo:hi, : d.width] = gk.astype(BF16)
+        r.x_out[lo:hi, d.width :] = gv.astype(BF16)
     cores[2].start()
 
     @pl.when(core == 0)
@@ -401,17 +383,17 @@
         for copy in own_back:
             copy.start()
 
-    each_head(d, lambda h: beacon_probs(r, d, h, 0))
-    gk, gv = beacon_grads(r, d, 0)
+    for lo, hi, gk, gv in beacon_grads(r, d, 0):
+        r.g_own[lo:hi, : d.width] = gk
+        r.g_own[lo:hi, d.width :] = gv
     cores[2].wait_recv()
 
     @pl.when(core == 1)
     def _():
         cores[3].wait_recv()
 
-    gk = gk + r.x_in[:, : d.width].astype(F32)
-    gv = gv + r.x_in[:, d.width :].astype(F32)
-    pack_halves(r.g_out, slice(None), gk, gv, half)
+    total = r.g_own[...] + r.x_in[...].astype(F32)
+    pack_halves(r.g_out, slice(None), total[:, : d.width], total[:, d.width :], half)
 
     def push_back(i, carry):
         k = window - i // 2
@@ -429,13 +411,11 @@
 
     lax.fori_loop(0, 2 * window, push_back, 0)
 
-    each_head(d, lambda h: raw_probs(r, d, h))
-    raw_key_grads(r, d, r.p_raw, r.do, r.gvt, 1.0)
-    r.gout[1] = r.gvt[their_rows, :].astype(BF16)
-    pair[3].start()
-    raw_key_grads(r, d, r.s_raw, r.q, r.gkt, d.scale)
-    r.gout[0] = r.gkt[their_rows, :].astype(BF16)
-    pair[2].start()
+    for copy, lo in zip(pair_back, raw_blocks):
+        raw_grads(r, d, lo)
+        r.gout[0, :, lo : lo + BLOCK] = r.gkt[their_rows, lo : lo + BLOCK].astype(BF16)
+        r.gout[1, :, lo : lo + BLOCK] = r.gvt[their_rows, lo : lo + BLOCK].astype(BF16)
+        copy.start()
 
     r.bkey[...] = r.bkv[:, : d.width].T
     for h in range(d.heads):
@@ -455,12 +435,12 @@
     r.gbk[...] = total[:, :half]
     r.gbv[...] = total[:, half:]
 
-    pair[3].wait_recv()
+    for copy in pair_back:
+        copy.wait_recv()
+    r.gk[...] = r.gkt[my_rows, :] + r.gin[0].astype(F32)
     r.gv[...] = r.gvt[my_rows, :] + r.gin[1].astype(F32)
-    pair[2].wait_recv()
-    r.gk[...] = r.gkt[my_rows, :] + r.gin[0].astype(F32)
-
-    for copy in pair:
+
+    for copy in pair + pair_back:
         copy.wait_send()
     cores[0].wait_send()
     cores[2].wait_send()
@@ -536,8 +516,6 @@
         e_b=vmem((d.heads, 2 * d.nb, d.span), F32),
         dp_raw=vmem((d.heads, d.span, d.span), F32),
         dp_b=vmem((d.heads, 2 * d.nb, d.span), F32),
-        p_raw=vmem((d.heads, d.span, d.span), BF16),
-        p_b=vmem((d.heads, 2 * d.nb, d.span), BF16),
         s_raw=vmem((d.heads, d.span, d.span), BF16),
         s_b=vmem((d.heads, 2 * d.nb, d.span), BF16),
         stats=vmem((d.heads, 16, d.span), F32),
@@ -548,11 +526,12 @@
         x_out=vmem((d.nb, 2 * d.width), BF16),
         x_in=vmem((d.nb, 2 * d.width), BF16),
         own_out=vmem((2, d.per, d.width), BF16),
+        g_own=vmem((d.nb, 2 * d.width), F32),
         g_out=vmem((2, d.nb, d.width), BF16),
         red=vmem((2, d.nb + d.per, d.width), BF16),
         load_sem=dma((8,)),
-        pair_send=dma((4,)),
-        pair_recv=dma((4,)),
+        pair_send=dma((6,)),
+        pair_recv=dma((6,)),
         core_send=dma((4,)),
         core_recv=dma((4,)),
         own_send=dma((2,)),
@@ -618,6 +597,7 @@
         in_specs=[vmem] * 5,
         out_specs=[hbm] * 5,
         scratch_shapes=[pltpu.SemaphoreType.DMA((5,))],
+        compiler_params=pltpu.CompilerParams(vmem_limit_bytes=2 * 1024 * 1024),
         name="write_out",
     )(*results)
     return (*results[:3], results[3].T, results[4].T)

time: 36.4 us -> 28.9 us (0.79)
  Pallas kernels: 32.3 us -> 28.1 us
  local copies, waits for them, and re-layouts: 3.27 us -> 0 us
    unnamed x10 -> x0, local copies, waits for them, and re-layouts: 3.27 us -> none
    pallas_call x1, Pallas kernels: 30.2 us -> 27.2 us  [on_device(): pl.pallas_call(functools.partial(kernel, IN_NAMES + OUT_NAMES + tuple(spa...]
    pallas_call x1, Pallas kernels: 2.07 us -> 0.92 us  [on_device(): pl.pallas_call(write_out, out_shape=shapes, in_specs=[vmem] * 5, out_spec...]
where the time goes in v3:
time: 28.9 us; the launch traced here: 28.8 us
  Pallas kernels  28.1 us (97%)
  between operations  0.64 us (2%)
    pallas_call x1, Pallas kernels, on_device(): pl.pallas_call(functools.partial(kernel, IN_NAMES + OUT_NAMES + tuple(spa...  27.2 us
    pallas_call x1, Pallas kernels, on_device(): pl.pallas_call(write_out, out_shape=shapes, in_specs=[vmem] * 5, out_spec...  0.92 us

profile of v3, /device:TPU:1, one launch (start us, length us, event | category | flops | bytes accessed | tf_op | source)
XLA Modules:
  0.0 28.8 jit_solution(4027836651423866220)
XLA Ops:
  0.6 27.2 %beacon_backward.1 = (bf16[512,512]{1,0:T(8,128)(2,1)S(1)}, f32[64,512]{1,0:T(8,128)S(1)}, f32[64,512]{1,0:T(8,128)S(1)}, f32[32,64]{1,0:T(8,128)S(1)}, f32[32,64]{1,0:T(8,128)S(1)}) custom-call(s32[32]{0:T(128)} %refs_0_.1, bf16[512,512]{1,0:T(8,128)(2,1)} %refs_1_.1, bf16[512,512]{1,0:T(8,128)(2,1)} %refs_2_.1, bf16[64,512]{1,0:T(8,128)(2,1)} %refs_3_.1, ...), custom_call_target="tpu_custom_call" | custom-call | flops 2684354560 | bytes 1572864 | tf_op jit(solution)/shard_map/beacon_backward/pallas_call | solution.py:578
  27.8 0.9 %write_out.1 = (bf16[512,512]{1,0:T(8,128)(2,1)}, f32[64,512]{1,0:T(8,128)}, f32[64,512]{1,0:T(8,128)}, f32[32,64]{1,0:T(8,128)}, f32[32,64]{1,0:T(8,128)}) custom-call(bf16[512,512]{1,0:T(8,128)(2,1)S(1)} %get-tuple-element.15.refs_0_, f32[64,512]{1,0:T(8,128)S(1)} %get-tuple-element.16.refs_1_, f32[64,512]{1,0:T(8,128)S(1)} %get-tuple-element.17.refs_2_, ...), custom_call_target="tpu_custom_call" | custom-call | tf_op jit(solution)/shard_map/write_out/pallas_call | solution.py:594

commit v4 on v3

v4 whole, which is shorter than its diff:
```python
import functools
import math
import types

import jax
import jax.numpy as jnp
from jax import lax
from jax.experimental import pallas as pl
from jax.experimental.pallas import tpu as pltpu
from jax.sharding import PartitionSpec as P

MESH = pl.DeviceIdType.MESH
F32 = jnp.float32
BF16 = jnp.bfloat16
HIDDEN = -1e30
BLOCK = 128
LOG2E = math.log2(math.e)


def dot(a, b):
    return lax.dot_general(a, b, (((1,), (0,)), ((), ())), preferred_element_type=F32)


def head_lanes(h, width):
    return slice(h * width, (h + 1) * width)


def turn_queries(r, d):
    for h in range(d.heads):
        r.qt[h] = r.q[:, head_lanes(h, d.width)].T
        r.dot_t[h] = r.do[:, head_lanes(h, d.width)].T


def hide_tokens(r, d):
    begin = r.turn[...].reshape(1, d.span)
    rows = lax.broadcasted_iota(jnp.int32, (BLOCK, d.span), 0)
    cols = lax.broadcasted_iota(jnp.int32, (BLOCK, d.span), 1)
    for lo in range(0, d.span, BLOCK):
        at = rows + lo
        seen = (at <= cols) & (at >= begin)
        r.bias[lo : lo + BLOCK, :] = jnp.where(seen, 0.0, HIDDEN)


def note(r, h, part, lo, top, e, g):
    rows = (top, jnp.sum(e, axis=0, keepdims=True), jnp.sum(e * g, axis=0, keepdims=True))
    for i, row in enumerate(rows):
        r.stats[h, 3 * part + i : 3 * part + i + 1, lo:] = row
        if lo:
            fill = jnp.full((1, lo), HIDDEN if i == 0 else 0.0, F32)
            r.stats[h, 3 * part + i : 3 * part + i + 1, :lo] = fill


def raw_part(r, d, h, part):
    lo, hi = part * BLOCK, (part + 1) * BLOCK
    s = dot(r.kt[lo:hi, :], r.qt[h, :, lo:]) * d.factor + r.bias[lo:hi, lo:]
    r.e_raw[h, lo:hi, lo:] = s
    top = jnp.max(s, axis=0, keepdims=True)
    e = jnp.exp2(r.e_raw[h, lo:hi, lo:] - top)
    r.e_raw[h, lo:hi, lo:] = e
    g = dot(r.vt[lo:hi, :], r.dot_t[h, :, lo:])
    r.dp_raw[h, lo:hi, lo:] = g
    note(r, h, part, lo, top, e, g)


def slot_shift(r, d, me, side, slot):
    core = lax.rem(me, 2)
    k = d.order[slot]
    if side == 0:
        span_id = me - 2 * k
    elif k < d.window:
        span_id = me + 1 - 2 * core - 2 * k
    else:
        span_id = me - core + (1 - core) * (1 - 2 * k)
    shown = (span_id >= 0) & (r.chat[jnp.maximum(span_id, 0)] == r.chat[me])
    return jnp.where(shown, 0.0, HIDDEN).astype(F32)


def part_of(d, side, group):
    first, end = d.groups[group]
    base = side * d.nb
    return d.raws + 2 * side + group, first, base + first * d.per, base + end * d.per


def beacon_part(r, d, h, side, group, shifts):
    part, _, lo, hi = part_of(d, side, group)
    top = jnp.full((1, d.span), HIDDEN, F32)
    s = dot(r.bkv[lo:hi, : d.width], r.qt[h]) * d.factor
    for i, shift in enumerate(shifts):
        moved = s[i * d.per : (i + 1) * d.per] + shift
        r.e_b[h, lo + i * d.per : lo + (i + 1) * d.per, :] = moved
        top = jnp.maximum(top, jnp.max(moved, axis=0, keepdims=True))
    e = jnp.exp2(r.e_b[h, lo:hi, :] - top)
    r.e_b[h, lo:hi, :] = e
    g = dot(r.bkv[lo:hi, d.width :], r.dot_t[h])
    r.dp_b[h, lo:hi, :] = g
    note(r, h, part, 0, top, e, g)


def combine(r, d, h):
    tops = [r.stats[h, 3 * i : 3 * i + 1, :] for i in range(d.parts)]
    top = functools.reduce(jnp.maximum, tops)
    factors = [jnp.exp2(t - top) for t in tops]
    total = jnp.zeros((1, d.span), F32)
    delta = jnp.zeros((1, d.span), F32)
    for i, f in enumerate(factors):
        total = total + f * r.stats[h, 3 * i + 1 : 3 * i + 2, :]
        delta = delta + f * r.stats[h, 3 * i + 2 : 3 * i + 3, :]
    inv = 1.0 / total
    for i, f in enumerate(factors):
        r.stats[h, d.factors + i : d.factors + i + 1, :] = f * inv
    r.stats[h, d.delta : d.delta + 1, :] = delta * inv


def beacon_grads(r, d, side, group):
    part, _, lo, hi = part_of(d, side, group)
    gk = jnp.zeros((hi - lo, d.width), F32)
    gv = jnp.zeros((hi - lo, d.width), F32)
    for h in range(d.heads):
        p = r.e_b[h, lo:hi, :] * r.stats[h, d.factors + part : d.factors + part + 1, :]
        s = (p * (r.dp_b[h, lo:hi, :] - r.stats[h, d.delta : d.delta + 1, :])).astype(BF16)
        r.s_b[h, lo:hi, :] = s
        gk = gk + dot(s, r.q[:, head_lanes(h, d.width)])
        gv = gv + dot(p.astype(BF16), r.do[:, head_lanes(h, d.width)])
    return gk * d.scale, gv


def pack_halves(ref, at, gk, gv, half):
    ref[0, at, :] = jnp.concatenate([gk[:, :half], gv[:, :half]], axis=1).astype(BF16)
    ref[1, at, :] = jnp.concatenate([gk[:, half:], gv[:, half:]], axis=1).astype(BF16)


def raw_grads(r, d, lo):
    hi = lo + BLOCK
    at = d.factors + lo // BLOCK
    gk = jnp.zeros((BLOCK, d.width), F32)
    gv = jnp.zeros((BLOCK, d.width), F32)
    for h in range(d.heads):
        p = r.e_raw[h, lo:hi, lo:] * r.stats[h, at : at + 1, lo:]
        s = (p * (r.dp_raw[h, lo:hi, lo:] - r.stats[h, d.delta : d.delta + 1, lo:])).astype(BF16)
        r.s_raw[h, lo:hi, lo:] = s
        if lo % (2 * BLOCK):
            r.s_raw[h, lo:hi, lo - BLOCK : lo] = jnp.zeros((BLOCK, BLOCK), BF16)
        gk = gk + dot(s, r.q[lo:, head_lanes(h, d.width)])
        gv = gv + dot(p.astype(BF16), r.do[lo:, head_lanes(h, d.width)])
    r.gkt[:, lo:hi] = (gk * d.scale).T
    r.gvt[:, lo:hi] = gv.T


def query_grads(r, d, h):
    for lo in range(0, d.span, 2 * BLOCK):
        hi = lo + 2 * BLOCK
        g = dot(r.kv[0, :, :hi], r.s_raw[h, :hi, lo:hi]) + dot(r.bkey[...], r.s_b[h, :, lo:hi])
        r.gq[lo:hi, head_lanes(h, d.width)] = (g * d.scale).T.astype(BF16)


def unfold(r, d, side, group, halves):
    _, _, lo, hi = part_of(d, side, group)
    at = slice(lo - side * d.nb, hi - side * d.nb)
    low, high = halves[0, at, :], halves[1, at, :]
    half = d.half
    r.bkv[lo:hi, :] = jnp.concatenate(
        [low[:, :half], high[:, :half], low[:, half:], high[:, half:]], axis=1
    )


def wait_for(ref, sem):
    pltpu.make_async_copy(ref, ref, sem).wait()


def kernel(names, d, *refs):
    r = types.SimpleNamespace(**dict(zip(names, refs)))
    per, half, window, n_ctx = d.per, d.half, d.window, d.n_ctx

    z = lax.axis_index("group")
    me = lax.axis_index("ctx")
    parity = lax.rem(z, 2)
    even = z - parity
    partner = z + 1 - 2 * parity
    core = lax.rem(me, 2)
    sibling = me + 1 - 2 * core
    chip = lax.div(me, 2)
    chips = n_ctx // 2
    my_rows = pl.ds(parity * half, half)
    their_rows = pl.ds((1 - parity) * half, half)
    near = pl.ds(0, d.groups[0][1] * per)
    far = pl.ds(d.groups[0][1] * per, (window - d.groups[0][1]) * per)
    first = pl.ds(0, per)
    shared = pl.ds(per, (d.groups[0][1] - 1) * per)
    beyond = pl.ds(window * per, per)

    barrier = pltpu.get_barrier_semaphore()

    def greet(group, ctx):
        pl.semaphore_signal(barrier, inc=1, device_id=(group, ctx), device_id_type=MESH)

    for k in reversed(d.order):

        @pl.when(chip >= k)
        def _():
            for p in range(2):
                greet(even + p, me - 2 * k)

    greet(partner, me)
    greet(z, sibling)
    greet(partner, sibling)

    loads = [
        pltpu.make_async_copy(src, dst, r.load_sem.at[i])
        for i, (src, dst) in enumerate(
            (
                (r.bk_hbm, r.bkhalf),
                (r.bv_hbm, r.bvhalf),
                (r.k_hbm, r.kv.at[0, my_rows]),
                (r.v_hbm, r.kv.at[1, my_rows]),
                (r.q_hbm, r.q),
                (r.do_hbm, r.do),
                (r.turn_hbm, r.turn),
                (r.chat_hbm, r.chat),
            )
        )
    ]
    for copy in loads:
        copy.start()

    loads[0].wait()
    loads[1].wait()
    r.beacon_out[...] = jnp.concatenate([r.bkhalf[...], r.bvhalf[...]], axis=1)
    loads[2].wait()
    loads[3].wait()
    pl.semaphore_wait(barrier, 2 * jnp.minimum(window, chips - 1 - chip) + 3)

    def remote(src, dst, send, recv, group, ctx):
        return pltpu.make_async_remote_copy(
            src_ref=src,
            dst_ref=dst,
            send_sem=send,
            recv_sem=recv,
            device_id=(group, ctx),
            device_id_type=MESH,
        )

    def to_partner(i, src, dst):
        return remote(src, dst, r.pair_send.at[i], r.pair_recv.at[i], partner, me)

    def to_sibling(i, src, dst):
        return remote(src, dst, r.core_send.at[i], r.core_recv.at[i], z, sibling)

    raw_blocks = range(0, d.span, BLOCK)
    pair = []
    pair_back = []
    mine = r.kv.at[:, my_rows]
    pair.append(to_partner(2 * d.raws, mine, mine))
    for i, lo in enumerate(raw_blocks):
        at = pl.ds(lo, BLOCK)
        pair_back.append(to_partner(d.raws + i, r.gout.at[:, :, at], r.gin.at[:, :, at]))
    cores = [
        to_sibling(0, r.b_in.at[:, shared], r.b_sib.at[:, shared]),
        to_sibling(1, r.b_in.at[:, first], r.b_sib.at[:, first]),
        to_sibling(2, r.b_in.at[:, far], r.b_sib.at[:, far]),
        to_sibling(3, r.x_out.at[far], r.x_in.at[far]),
        to_sibling(4, r.x_out.at[shared], r.x_in.at[shared]),
        to_sibling(5, r.x_out.at[first], r.x_in.at[first]),
    ]


    def push(group):
        for slot in reversed(range(*d.groups[group])):
            k = d.order[slot]

            @pl.when(chip + k < chips)
            def _():
                for p in range(2):
                    remote(
                        r.beacon_out,
                        r.b_in.at[parity, pl.ds(slot * per, per)],
                        r.b_send.at[slot],
                        r.b_recv.at[slot],
                        even + p,
                        me + 2 * k,
                    ).start()

    push(1)
    push(0)
    pair[0].start()

    own_chip = [
        remote(
            r.beacon_out,
            r.b_sib.at[parity, first],
            r.own_send.at[i],
            r.own_recv,
            group,
            sibling,
        )
        for i, group in enumerate((z, partner))
    ]

    @pl.when(core == 0)
    def _():
        for copy in own_chip:
            copy.start()

    for i in (4, 5, 6, 7):
        loads[i].wait()
    turn_queries(r, d)
    hide_tokens(r, d)

    @pl.when(core == 0)
    def _():
        r.x_in[first, :] = jnp.zeros((per, 2 * d.width), BF16)

    @pl.when(core == 1)
    def _():
        r.red[:, beyond, :] = jnp.zeros((2, per, d.width), BF16)

    nothing = jnp.zeros((2, per, d.width), BF16)
    for slot in range(window):
        k = d.order[slot]
        at = pl.ds(slot * per, per)

        @pl.when(chip < k)
        def _():
            r.b_in[:, at, :] = nothing

        @pl.when(chip + k >= chips)
        def _():
            r.red[:, at, :] = nothing


    def shifts(side, group):
        return [slot_shift(r, d, me, side, slot) for slot in range(*d.groups[group])]

    def attend(side, group, halves):
        unfold(r, d, side, group, halves)
        moves = shifts(side, group)
        for h in range(d.heads):
            beacon_part(r, d, h, side, group, moves)

    def raw(part):
        if part == 0:
            pair[0].wait_recv()
        lo, hi = part * BLOCK, (part + 1) * BLOCK
        r.kt[lo:hi, :] = r.kv[0, :, lo:hi].T
        r.vt[lo:hi, :] = r.kv[1, :, lo:hi].T
        for h in range(d.heads):
            raw_part(r, d, h, part)

    def slot_rows(slot):
        return pl.ds(slot * per, per)

    def arrived(group):
        for slot in range(*d.groups[group]):

            @pl.when(chip >= d.order[slot])
            def _():
                wait_for(r.b_in.at[:, slot_rows(slot)], r.b_recv.at[slot])

    def exchange_near():
        arrived(0)
        cores[0].start()

        @pl.when(core == 1)
        def _():
            cores[1].start()

    def exchange_far():
        arrived(1)
        cores[2].start()

    def near_from_sibling():
        cores[0].wait_recv()

        @pl.when(core == 0)
        def _():
            cores[1].wait_recv()

        @pl.when(core == 1)
        def _():
            wait_for(r.b_sib.at[:, first], r.own_recv)

        attend(1, 0, r.b_sib)

    exchange_near()
    exchange_far()
    attend(0, 0, r.b_in)
    attend(0, 1, r.b_in)
    raw(0)
    raw(1)
    near_from_sibling()
    cores[2].wait_recv()
    attend(1, 1, r.b_sib)
    raw(2)
    raw(3)
    for h in range(d.heads):
        combine(r, d, h)

    def to_other_core(group):
        _, _, lo, hi = part_of(d, 0, group)
        gk, gv = beacon_grads(r, d, 1, group)
        r.x_out[lo:hi, : d.width] = gk.astype(BF16)
        r.x_out[lo:hi, d.width :] = gv.astype(BF16)

    own_back = [
        remote(
            r.own_out.at[p],
            r.red.at[parity, beyond],
            r.back_send.at[p],
            r.back_recv,
            even + p,
            sibling,
        )
        for p in range(2)
    ]


    def to_owners(group):
        _, _, lo, hi = part_of(d, 0, group)
        gk = r.g_own[lo:hi, : d.width] + r.x_in[lo:hi, : d.width].astype(F32)
        gv = r.g_own[lo:hi, d.width :] + r.x_in[lo:hi, d.width :].astype(F32)
        pack_halves(r.g_out, slice(lo, hi), gk, gv, half)
        for slot in reversed(range(*d.groups[group])):
            k = d.order[slot]

            @pl.when(chip >= k)
            def _():
                at = pl.ds(slot * per, per)
                for p in range(2):
                    remote(
                        r.g_out.at[p, at],
                        r.red.at[parity, at],
                        r.g_send.at[slot],
                        r.g_recv.at[slot],
                        even + p,
                        me - 2 * k,
                    ).start()

    def raw_back(part):
        lo = part * BLOCK
        raw_grads(r, d, lo)
        r.gout[0, :, lo : lo + BLOCK] = r.gkt[their_rows, lo : lo + BLOCK].astype(BF16)
        r.gout[1, :, lo : lo + BLOCK] = r.gvt[their_rows, lo : lo + BLOCK].astype(BF16)
        pair_back[part].start()

    def far_to_sibling():
        to_other_core(1)
        cores[3].start()

    def near_to_sibling():
        to_other_core(0)
        cores[4].start()

        @pl.when(core == 0)
        def _():
            cores[5].start()

        own = r.x_out[first, :]
        pack_halves(r.own_out, slice(None), own[:, : d.width], own[:, d.width :], half)

        @pl.when(core == 1)
        def _():
            for copy in own_back:
                copy.start()

    def own_grads(group):
        _, _, lo, hi = part_of(d, 0, group)
        gk, gv = beacon_grads(r, d, 0, group)
        r.g_own[lo:hi, : d.width] = gk
        r.g_own[lo:hi, d.width :] = gv

    def far_to_owners():
        cores[3].wait_recv()
        to_owners(1)

    def near_to_owners():
        cores[4].wait_recv()

        @pl.when(core == 1)
        def _():
            cores[5].wait_recv()

        to_owners(0)

    far_to_sibling()
    near_to_sibling()
    own_grads(1)
    far_to_owners()
    raw_back(0)
    own_grads(0)
    near_to_owners()
    raw_back(1)
    raw_back(2)
    raw_back(3)

    r.bkey[...] = r.bkv[:, : d.width].T
    for h in range(d.heads):
        query_grads(r, d, h)

    for slot in range(window):

        @pl.when(chip + d.order[slot] < chips)
        def _():
            wait_for(r.red.at[:, slot_rows(slot)], r.g_recv.at[slot])


    @pl.when(core == 0)
    def _():
        wait_for(r.red.at[:, beyond], r.back_recv)

    total = jnp.zeros((per, d.width), F32)
    for p in range(2):
        for k in range(window + 1):
            total = total + r.red[p, k * per : (k + 1) * per, :].astype(F32)
    r.gbk[...] = total[:, :half]
    r.gbv[...] = total[:, half:]

    for copy in pair_back:
        copy.wait_recv()
    r.gk[...] = r.gkt[my_rows, :] + r.gin[0].astype(F32)
    r.gv[...] = r.gvt[my_rows, :] + r.gin[1].astype(F32)

    for copy in pair + pair_back:
        copy.wait_send()
    for i in (0, 2, 3, 4):
        cores[i].wait_send()

    @pl.when(core == 0)
    def _():
        cores[5].wait_send()
        for copy in own_chip:
            copy.wait_send()

    @pl.when(core == 1)
    def _():
        cores[1].wait_send()
        for copy in own_back:
            copy.wait_send()

    for slot in range(window):
        k = d.order[slot]

        @pl.when(chip + k < chips)
        def _():
            wait_for(r.b_in.at[:, slot_rows(slot)], r.b_send.at[slot])

        @pl.when(chip >= k)
        def _():
            wait_for(r.g_out.at[:, slot_rows(slot)], r.g_send.at[slot])


def write_out(*refs):
    sources, results, sems = refs[:5], refs[5:10], refs[10]
    copies = [
        pltpu.make_async_copy(s, o, sems.at[i]) for i, (s, o) in enumerate(zip(sources, results))
    ]
    for copy in copies:
        copy.start()
    for copy in copies:
        copy.wait()


def dims(n_ctx, span, lanes, half, per):
    width = 2 * half
    window = min(8, n_ctx // 2 - 1)
    order = tuple(sorted(range(1, window + 1), key=lambda k: (k != window, (4, 1, 3, 2, 5, 7, 6, 8).index(k))))
    near = (window + 1) // 2
    raws = span // BLOCK
    return types.SimpleNamespace(
        n_ctx=n_ctx,
        span=span,
        lanes=lanes,
        half=half,
        per=per,
        width=width,
        heads=lanes // width,
        window=window,
        nb=window * per,
        order=order,
        groups=((0, near), (near, window)),
        raws=raws,
        parts=raws + 4,
        factors=3 * (raws + 4),
        delta=4 * (raws + 4),
        scale=width ** (-0.5),
        factor=width ** (-0.5) * LOG2E,
    )


def scratch(d):
    vmem = pltpu.VMEM
    dma = pltpu.SemaphoreType.DMA
    return dict(
        q=vmem((d.span, d.lanes), BF16),
        do=vmem((d.span, d.lanes), BF16),
        bkhalf=vmem((d.per, d.half), BF16),
        bvhalf=vmem((d.per, d.half), BF16),
        turn=vmem((d.span,), jnp.int32),
        chat=pltpu.SMEM((d.n_ctx,), jnp.int32),
        qt=vmem((d.heads, d.width, d.span), BF16),
        dot_t=vmem((d.heads, d.width, d.span), BF16),
        bias=vmem((d.span, d.span), F32),
        kv=vmem((2, d.width, d.span), BF16),
        kt=vmem((d.span, d.width), BF16),
        vt=vmem((d.span, d.width), BF16),
        beacon_out=vmem((d.per, d.width), BF16),
        b_in=vmem((2, d.nb, d.width), BF16),
        b_sib=vmem((2, d.nb, d.width), BF16),
        bkv=vmem((2 * d.nb, 2 * d.width), BF16),
        bkey=vmem((d.width, 2 * d.nb), BF16),
        e_raw=vmem((d.heads, d.span, d.span), F32),
        e_b=vmem((d.heads, 2 * d.nb, d.span), F32),
        dp_raw=vmem((d.heads, d.span, d.span), F32),
        dp_b=vmem((d.heads, 2 * d.nb, d.span), F32),
        s_raw=vmem((d.heads, d.span, d.span), BF16),
        s_b=vmem((d.heads, 2 * d.nb, d.span), BF16),
        stats=vmem((d.heads, 8 * (d.parts // 2 + 1), d.span), F32),
        gkt=vmem((d.width, d.span), F32),
        gvt=vmem((d.width, d.span), F32),
        gout=vmem((2, d.half, d.span), BF16),
        gin=vmem((2, d.half, d.span), BF16),
        x_out=vmem((d.nb, 2 * d.width), BF16),
        x_in=vmem((d.nb, 2 * d.width), BF16),
        own_out=vmem((2, d.per, d.width), BF16),
        g_own=vmem((d.nb, 2 * d.width), F32),
        g_out=vmem((2, d.nb, d.width), BF16),
        red=vmem((2, d.nb + d.per, d.width), BF16),
        load_sem=dma((8,)),
        pair_send=dma((2 * d.raws + 1,)),
        pair_recv=dma((2 * d.raws + 1,)),
        core_send=dma((6,)),
        core_recv=dma((6,)),
        own_send=dma((2,)),
        own_recv=dma,
        back_send=dma((2,)),
        back_recv=dma,
        b_send=dma((d.window,)),
        b_recv=dma((d.window,)),
        g_send=dma((d.window,)),
        g_recv=dma((d.window,)),
    )


IN_NAMES = ("chat_hbm", "q_hbm", "do_hbm", "k_hbm", "v_hbm", "bk_hbm", "bv_hbm", "turn_hbm")
OUT_NAMES = ("gq", "gk", "gv", "gbk", "gbv")


def on_device(
    n_ctx, query, grad_out, key_raw, value_raw, beacon_key, beacon_value, chat_of_span, turn_begin
):
    span, lanes = query.shape
    half, per = beacon_key.shape
    d = dims(n_ctx, span, lanes, half, per)
    space = scratch(d)
    hbm = pl.BlockSpec(memory_space=pltpu.HBM)
    vmem = pl.BlockSpec(memory_space=pltpu.VMEM)
    shapes = (
        jax.ShapeDtypeStruct((span, lanes), BF16),
        jax.ShapeDtypeStruct((half, span), F32),
        jax.ShapeDtypeStruct((half, span), F32),
        jax.ShapeDtypeStruct((per, half), F32),
        jax.ShapeDtypeStruct((per, half), F32),
    )
    operands = (
        chat_of_span,
        query,
        grad_out,
        key_raw,
        value_raw,
        beacon_key.T,
        beacon_value.T,
        turn_begin,
    )
    results = pl.pallas_call(
        functools.partial(kernel, IN_NAMES + OUT_NAMES + tuple(space), d),
        out_shape=shapes,
        in_specs=[hbm] * 8,
        out_specs=[vmem] * 5,
        scratch_shapes=list(space.values()),
        compiler_params=pltpu.CompilerParams(
            collective_id=0, has_side_effects=True, vmem_limit_bytes=48 * 1024 * 1024
        ),
        cost_estimate=pl.CostEstimate(
            flops=10 * d.heads * span * (span + 2 * d.nb) * d.width,
            bytes_accessed=6 * span * lanes,
            transcendentals=d.heads * span * (span + 2 * d.nb),
        ),
        name="beacon_backward",
    )(*[pltpu.with_memory_space_constraint(a, pltpu.HBM) for a in operands])
    results = pl.pallas_call(
        write_out,
        out_shape=shapes,
        in_specs=[vmem] * 5,
        out_specs=[hbm] * 5,
        scratch_shapes=[pltpu.SemaphoreType.DMA((5,))],
        compiler_params=pltpu.CompilerParams(vmem_limit_bytes=2 * 1024 * 1024),
        name="write_out",
    )(*results)
    return (*results[:3], results[3].T, results[4].T)


def solution(mesh):
    in_specs = (
        P("ctx", "group"),
        P("ctx", "group"),
        P("group", "ctx"),
        P("group", "ctx"),
        P("group", "ctx"),
        P("group", "ctx"),
        P(),
        P("ctx"),
    )
    out_specs = (
        P("ctx", "group"),
        P("group", "ctx"),
        P("group", "ctx"),
        P("group", "ctx"),
        P("group", "ctx"),
    )
    return jax.shard_map(
        functools.partial(on_device, mesh.shape["ctx"]),
        mesh=mesh,
        in_specs=in_specs,
        out_specs=out_specs,
        check_vma=False,
    )
```

time: 28.9 us -> 26.4 us (0.913)
  Pallas kernels: 28.1 us -> 25.6 us
    pallas_call x1, Pallas kernels: 27.2 us -> 24.6 us  [on_device(): pl.pallas_call(functools.partial(kernel, IN_NAMES + OUT_NAMES + tuple(spa...]
where the time goes in v4:
time: 26.4 us; the launch traced here: 26.2 us
  Pallas kernels  25.6 us (97%)
  between operations  0.64 us (2%)
    pallas_call x1, Pallas kernels, on_device(): pl.pallas_call(functools.partial(kernel, IN_NAMES + OUT_NAMES + tuple(spa...  24.6 us
    pallas_call x1, Pallas kernels, on_device(): pl.pallas_call(write_out, out_shape=shapes, in_specs=[vmem] * 5, out_spec...  0.92 us

profile of v4, /device:TPU:1, one launch (start us, length us, event | category | flops | bytes accessed | tf_op | source)
XLA Modules:
  0.0 26.2 jit_solution(18188147977760369853)
XLA Ops:
  0.6 24.6 %beacon_backward.1 = (bf16[512,512]{1,0:T(8,128)(2,1)S(1)}, f32[64,512]{1,0:T(8,128)S(1)}, f32[64,512]{1,0:T(8,128)S(1)}, f32[32,64]{1,0:T(8,128)S(1)}, f32[32,64]{1,0:T(8,128)S(1)}) custom-call(s32[32]{0:T(128)} %refs_0_.1, bf16[512,512]{1,0:T(8,128)(2,1)} %refs_1_.1, bf16[512,512]{1,0:T(8,128)(2,1)} %refs_2_.1, bf16[64,512]{1,0:T(8,128)(2,1)} %refs_3_.1, ...), custom_call_target="tpu_custom_call" | custom-call | flops 2684354560 | bytes 1572864 | tf_op jit(solution)/shard_map/beacon_backward/pallas_call | solution.py:672
  25.3 0.9 %write_out.1 = (bf16[512,512]{1,0:T(8,128)(2,1)}, f32[64,512]{1,0:T(8,128)}, f32[64,512]{1,0:T(8,128)}, f32[32,64]{1,0:T(8,128)}, f32[32,64]{1,0:T(8,128)}) custom-call(bf16[512,512]{1,0:T(8,128)(2,1)S(1)} %get-tuple-element.15.refs_0_, f32[64,512]{1,0:T(8,128)S(1)} %get-tuple-element.16.refs_1_, f32[64,512]{1,0:T(8,128)S(1)} %get-tuple-element.17.refs_2_, ...), custom_call_target="tpu_custom_call" | custom-call | tf_op jit(solution)/shard_map/write_out/pallas_call | solution.py:688

commit v5 on v4

--- a/solution.py
+++ b/solution.py
@@ -188,22 +188,6 @@
     shared = pl.ds(per, (d.groups[0][1] - 1) * per)
     beyond = pl.ds(window * per, per)
 
-    barrier = pltpu.get_barrier_semaphore()
-
-    def greet(group, ctx):
-        pl.semaphore_signal(barrier, inc=1, device_id=(group, ctx), device_id_type=MESH)
-
-    for k in reversed(d.order):
-
-        @pl.when(chip >= k)
-        def _():
-            for p in range(2):
-                greet(even + p, me - 2 * k)
-
-    greet(partner, me)
-    greet(z, sibling)
-    greet(partner, sibling)
-
     loads = [
         pltpu.make_async_copy(src, dst, r.load_sem.at[i])
         for i, (src, dst) in enumerate(
@@ -219,14 +203,31 @@
             )
         )
     ]
-    for copy in loads:
+    for copy in loads[:2]:
+        copy.start()
+
+    barrier = pltpu.get_barrier_semaphore()
+
+    def greet(group, ctx):
+        pl.semaphore_signal(barrier, inc=1, device_id=(group, ctx), device_id_type=MESH)
+
+    for k in reversed(d.order):
+
+        @pl.when(chip >= k)
+        def _():
+            for p in range(2):
+                greet(even + p, me - 2 * k)
+
+    greet(partner, me)
+    greet(z, sibling)
+    greet(partner, sibling)
+
+    for copy in loads[2:]:
         copy.start()
 
     loads[0].wait()
     loads[1].wait()
     r.beacon_out[...] = jnp.concatenate([r.bkhalf[...], r.bvhalf[...]], axis=1)
-    loads[2].wait()
-    loads[3].wait()
     pl.semaphore_wait(barrier, 2 * jnp.minimum(window, chips - 1 - chip) + 3)
 
     def remote(src, dst, send, recv, group, ctx):
@@ -281,6 +282,8 @@
 
     push(1)
     push(0)
+    loads[2].wait()
+    loads[3].wait()
     pair[0].start()
 
     own_chip = [
@@ -381,12 +384,12 @@
         attend(1, 0, r.b_sib)
 
     exchange_near()
+    attend(0, 0, r.b_in)
     exchange_far()
-    attend(0, 0, r.b_in)
     attend(0, 1, r.b_in)
+    near_from_sibling()
     raw(0)
     raw(1)
-    near_from_sibling()
     cores[2].wait_recv()
     attend(1, 1, r.b_sib)
     raw(2)
@@ -481,8 +484,8 @@
         to_owners(0)
 
     far_to_sibling()
+    own_grads(1)
     near_to_sibling()
-    own_grads(1)
     far_to_owners()
     raw_back(0)
     own_grads(0)

time: 26.4 us -> 26.1 us (0.989)
  Pallas kernels: 25.6 us -> 25.3 us
where the time goes in v5:
time: 26.1 us; the launch traced here: 26 us
  Pallas kernels  25.3 us (97%)
  between operations  0.64 us (2%)
    pallas_call x1, Pallas kernels, on_device(): pl.pallas_call(functools.partial(kernel, IN_NAMES + OUT_NAMES + tuple(spa...  24.4 us
    pallas_call x1, Pallas kernels, on_device(): pl.pallas_call(write_out, out_shape=shapes, in_specs=[vmem] * 5, out_spec...  0.92 us

profile of v5, /device:TPU:1, one launch (start us, length us, event | category | flops | bytes accessed | tf_op | source)
XLA Modules:
  0.0 26.0 jit_solution(201754980401416130)
XLA Ops:
  0.6 24.4 %beacon_backward.1 = (bf16[512,512]{1,0:T(8,128)(2,1)S(1)}, f32[64,512]{1,0:T(8,128)S(1)}, f32[64,512]{1,0:T(8,128)S(1)}, f32[32,64]{1,0:T(8,128)S(1)}, f32[32,64]{1,0:T(8,128)S(1)}) custom-call(s32[32]{0:T(128)} %refs_0_.1, bf16[512,512]{1,0:T(8,128)(2,1)} %refs_1_.1, bf16[512,512]{1,0:T(8,128)(2,1)} %refs_2_.1, bf16[64,512]{1,0:T(8,128)(2,1)} %refs_3_.1, ...), custom_call_target="tpu_custom_call" | custom-call | flops 2684354560 | bytes 1572864 | tf_op jit(solution)/shard_map/beacon_backward/pallas_call | solution.py:675
  25.1 0.9 %write_out.1 = (bf16[512,512]{1,0:T(8,128)(2,1)}, f32[64,512]{1,0:T(8,128)}, f32[64,512]{1,0:T(8,128)}, f32[32,64]{1,0:T(8,128)}, f32[32,64]{1,0:T(8,128)}) custom-call(bf16[512,512]{1,0:T(8,128)(2,1)S(1)} %get-tuple-element.15.refs_0_, f32[64,512]{1,0:T(8,128)S(1)} %get-tuple-element.16.refs_1_, f32[64,512]{1,0:T(8,128)S(1)} %get-tuple-element.17.refs_2_, ...), custom_call_target="tpu_custom_call" | custom-call | tf_op jit(solution)/shard_map/write_out/pallas_call | solution.py:691

commit v6 on v5

--- a/solution.py
+++ b/solution.py
@@ -390,10 +390,10 @@
     near_from_sibling()
     raw(0)
     raw(1)
+    raw(2)
+    raw(3)
     cores[2].wait_recv()
     attend(1, 1, r.b_sib)
-    raw(2)
-    raw(3)
     for h in range(d.heads):
         combine(r, d, h)
 

time: 26.1 us -> 26.1 us (level)
  no operation moved by 1% of the time
where the time goes in v6:
time: 26.1 us; the launch traced here: 26 us
  Pallas kernels  25.3 us (97%)
  between operations  0.64 us (2%)
    pallas_call x1, Pallas kernels, on_device(): pl.pallas_call(functools.partial(kernel, IN_NAMES + OUT_NAMES + tuple(spa...  24.4 us
    pallas_call x1, Pallas kernels, on_device(): pl.pallas_call(write_out, out_shape=shapes, in_specs=[vmem] * 5, out_spec...  0.92 us

profile of v6, /device:TPU:1, one launch (start us, length us, event | category | flops | bytes accessed | tf_op | source)
XLA Modules:
  0.0 26.0 jit_solution(1069963338439352648)
XLA Ops:
  0.6 24.4 %beacon_backward.1 = (bf16[512,512]{1,0:T(8,128)(2,1)S(1)}, f32[64,512]{1,0:T(8,128)S(1)}, f32[64,512]{1,0:T(8,128)S(1)}, f32[32,64]{1,0:T(8,128)S(1)}, f32[32,64]{1,0:T(8,128)S(1)}) custom-call(s32[32]{0:T(128)} %refs_0_.1, bf16[512,512]{1,0:T(8,128)(2,1)} %refs_1_.1, bf16[512,512]{1,0:T(8,128)(2,1)} %refs_2_.1, bf16[64,512]{1,0:T(8,128)(2,1)} %refs_3_.1, ...), custom_call_target="tpu_custom_call" | custom-call | flops 2684354560 | bytes 1572864 | tf_op jit(solution)/shard_map/beacon_backward/pallas_call | solution.py:675
  25.1 0.9 %write_out.1 = (bf16[512,512]{1,0:T(8,128)(2,1)}, f32[64,512]{1,0:T(8,128)}, f32[64,512]{1,0:T(8,128)}, f32[32,64]{1,0:T(8,128)}, f32[32,64]{1,0:T(8,128)}) custom-call(bf16[512,512]{1,0:T(8,128)(2,1)S(1)} %get-tuple-element.15.refs_0_, f32[64,512]{1,0:T(8,128)S(1)} %get-tuple-element.16.refs_1_, f32[64,512]{1,0:T(8,128)S(1)} %get-tuple-element.17.refs_2_, ...), custom_call_target="tpu_custom_call" | custom-call | tf_op jit(solution)/shard_map/write_out/pallas_call | solution.py:691
